TPU v7x, 32 devices: a whole 2x2x4 slice. The times are simulated.
32 devices in a mesh: groups: 2 (over x), row: 8 (over z, y), col: 2 (over core).
Axes of the slice: x: 2, y: 2, z: 4, core: 2. Of those that a mesh axis runs over, the one named last changes fastest.
Arguments:
- tokens: bfloat16 [1024, 8192], P(('groups', 'row'), 'col'), parts along dimension 0, may hold values from -6 to 6
- gate_weight: bfloat16 [8192, 14336], P('col', 'row'), may hold values from -0.125 to 0.125
- up_weight: bfloat16 [8192, 14336], P('col', 'row'), may hold values from -0.125 to 0.125
- down_weight: bfloat16 [14336, 8192], P('row', 'col'), may hold values from -0.09375 to 0.09375
- gate_mask: int32 [64, 112], P('col', 'row'), may hold values from 0 to 1, as said below
- up_mask: int32 [64, 112], P('col', 'row'), may hold values from 0 to 1, as said below
- down_mask: int32 [112, 64], P('row', 'col'), may hold values from 0 to 1, as said below
Outputs:
- mixed: bfloat16 [1024, 8192], P(('groups', 'row'), 'col'), parts along dimension 0
There are 2 independent parts, one for each index of `groups`. A program takes and returns all parts, laid end to end along the dimension named above; an argument that names none is the same for every part. Nothing has to cross between parts.
Inputs may be any that keep to these rules, and one draw needn't show every extreme that they name: `gate_mask`: 1 keeps the 128 x 128 block of the matching projection, 0 prunes it. `up_mask`: 1 keeps the 128 x 128 block of the matching projection, 0 prunes it. `down_mask`: 1 keeps the 128 x 128 block of the matching projection, 0 prunes it.
All inputs are finite; a program needn't handle non-finite values.
Results may differ from a plain program's by a relative error of at most 0.0049.
Values may be sent and summed in bfloat16 or wider, within the bound.
No kernel may reach another device: no remote copies, remote signals or barrier semaphores. Data moves between devices by JAX's collectives and lax.ppermute only.
A program may use at most 192 MiB of HBM per device.

v0:
```python
import jax
import jax.numpy as jnp
from jax import lax
from jax.sharding import PartitionSpec as P


def expand_mask(mask, weight):
    blocks_down, blocks_across = mask.shape
    side_down = weight.shape[0] // blocks_down
    side_across = weight.shape[1] // blocks_across
    spread = jnp.broadcast_to(
        mask[:, None, :, None], (blocks_down, side_down, blocks_across, side_across)
    )
    return weight * spread.reshape(weight.shape).astype(weight.dtype)


def gated(sums, width):
    return (jax.nn.silu(sums[:, :width]) * sums[:, width:]).astype(jnp.bfloat16)


def body(tokens, gate_weight, up_weight, down_weight, gate_mask, up_mask, down_mask):
    width = gate_weight.shape[1]
    both_kept = jnp.concatenate(
        (expand_mask(gate_mask, gate_weight), expand_mask(up_mask, up_weight)), axis=1
    )
    down_kept = expand_mask(down_mask, down_weight)
    partial_sums = jnp.dot(
        lax.all_gather(tokens, "row", axis=0, tiled=True),
        both_kept,
        preferred_element_type=jnp.float32,
    )
    summed = lax.psum(partial_sums, "col")
    hidden = gated(summed, width)
    mixed = lax.psum_scatter(
        jnp.dot(hidden, down_kept, preferred_element_type=jnp.float32),
        "row",
        scatter_dimension=0,
        tiled=True,
    )
    return mixed.astype(jnp.bfloat16)


def solution(mesh):
    return jax.shard_map(
        body,
        mesh=mesh,
        in_specs=(
            P(("groups", "row"), "col"),
            P("col", "row"),
            P("col", "row"),
            P("row", "col"),
            P("col", "row"),
            P("col", "row"),
            P("row", "col"),
        ),
        out_specs=P(("groups", "row"), "col"),
        check_vma=False,
    )
```

profile of v0, /device:TPU:0, one launch (start us, length us, event | category | flops | bytes accessed | tf_op | source)
XLA Modules:
  0.0 340.6 jit_solution(4105624384469482558)
XLA Ops:
  6.5 0.0 all-gather.2.cloned.1.call-start
  6.5 0.7 all-gather.2.cloned.1.call-update
  7.3 0.0 all-reduce.2.cloned.1.call-start
  7.3 0.7 convert_element_type.27
  8.0 0.7 convert_element_type.29
  8.7 20.2 %copy.10 = bf16[4096,1792]{0,1:T(8,128)(2,1)} copy(bf16[4096,1792]{1,0:T(8,128)(2,1)} %param.8) | data formatting | bytes 29360128 | tf_op args[1]
  28.9 19.6 %copy.11 = bf16[4096,1792]{0,1:T(8,128)(2,1)} copy(bf16[4096,1792]{1,0:T(8,128)(2,1)} %param.9) | data formatting | bytes 29360128 | tf_op args[2]
  48.6 7.2 %broadcast_in_dim.6 = bf16[32,128,14,128]{1,0,3,2:T(8,128)(2,1)} broadcast(bf16[32,14]{0,1:T(8,128)(2,1)S(1)} %convert_element_type.27), dimensions={0,2} | broadcast | bytes 14680960 | tf_op jit(solution)/shard_map/broadcast_in_dim | solution.py:11
  55.7 7.2 %broadcast_in_dim.7 = bf16[32,128,14,128]{1,0,3,2:T(8,128)(2,1)} broadcast(bf16[32,14]{0,1:T(8,128)(2,1)S(1)} %convert_element_type.29), dimensions={0,2} | broadcast | bytes 14680960 | tf_op jit(solution)/shard_map/broadcast_in_dim | solution.py:11
  62.9 33.7 %bitcast_multiply_fusion.2 = (bf16[4096,1792]{0,1:T(8,128)(2,1)}, bf16[4096,1792]{0,1:T(8,128)(2,1)}) fusion(bf16[4096,1792]{0,1:T(8,128)(2,1)} %copy.11, bf16[224,8,32,128]{3,2,1,0:T(8,128)(2,1)} %bitcast.21, bf16[4096,1792]{0,1:T(8,128)(2,1)} %copy.10, bf16[224,8,32,128]{3,2,1,0:T(8,128)(2,1)} %bitcast.20), kind=kLoop, calls=%fused_computation.7 | loop fusion | flops 14680064 | bytes 88080384 | tf_op jit(solution)/shard_map/mul | solution.py:14
  96.6 0.0 all-gather.2.cloned.1.call-done
  96.6 0.0 copy-start
  96.6 22.5 %fusion.6 = f32[512,3584]{0,1:T(8,128)} fusion(bf16[512,4096]{1,0:T(8,128)(2,1)} %all-gather.2.cloned.1.call-done, bf16[4096,1792]{0,1:T(8,128)(2,1)} %get-tuple-element.5, bf16[4096,1792]{0,1:T(8,128)(2,1)} %get-tuple-element.6), kind=kOutput, calls=%fused_computation.9 | convolution fusion | flops 15091105792 | bytes 40894464 | tf_op jit(solution)/shard_map/dot_general | solution.py:27
  119.1 0.0 all-reduce.2.cloned.1.call-update
  119.1 0.2 reduce-scatter.2.cloned.1.call-start
  119.3 0.0 copy-done
  119.4 36.7 %all-reduce.2.cloned.1.call-done = f32[512,3584]{0,1:T(8,128)} async-done(((f32[512,3584]{0,1:T(8,128)}), f32[512,3584]{0,1:T(8,128)}) %all-reduce.2.cloned.1.call-update) | async-done | bytes 7340048 | tf_op jit(solution)/shard_map/psum | solution.py:32
  156.1 7.2 %broadcast_in_dim.8 = bf16[14,128,32,128]{3,2,1,0:T(8,128)(2,1)} broadcast(bf16[14,32]{1,0:T(8,128)(2,1)S(1)} %convert_element_type.32), dimensions={0,2} | broadcast | bytes 14680960 | tf_op jit(solution)/shard_map/broadcast_in_dim | solution.py:11
  163.2 18.4 %fusion.4 = f32[512,4096]{1,0:T(8,128)} fusion(bf16[1792,4096]{1,0:T(8,128)(2,1)} %param.10, bf16[224,8,32,128]{3,2,1,0:T(8,128)(2,1)} %bitcast.22, f32[512,3584]{0,1:T(8,128)} %all-reduce.2.cloned.1.call-done), kind=kOutput, calls=%fused_computation.5 | convolution fusion | flops 7529037824 | bytes 45088768 | tf_op jit(solution)/shard_map/dot_general | solution.py:35
  181.6 0.0 reduce-scatter.2.cloned.1.call-update
  181.7 150.4 %reduce-scatter.2.cloned.1.call-done = f32[64,4096]{1,0:T(8,128)} async-done(((f32[512,4096]{1,0:T(8,128)}), f32[64,4096]{1,0:T(8,128)}) %reduce-scatter.2.cloned.1.call-update) | async-done | bytes 1048592 | tf_op jit(solution)/shard_map/reduce_scatter | solution.py:34
  332.0 2.1 convert_element_type.34
  (1 shorter events, 0.0 us)
Async XLA Ops:
  6.5 90.1 %all-gather.2.cloned.1.call-start = ((), (), s32[]{:S(2)}) async-start(), calls=%async_computation.1 | async-start | bytes 4718592 | tf_op jit(solution)/shard_map/all_gather | solution.py:28
  7.3 148.8 %all-reduce.2.cloned.1.call-start = ((), (), s32[]{:S(2)}) async-start(), calls=%async_computation.2 | async-start | bytes 14680064 | tf_op jit(solution)/shard_map/psum | solution.py:32
  96.6 22.8 %copy-start = (s32[14,32]{1,0:T(8,128)S(1)}, s32[14,32]{1,0:T(8,128)}, u32[]{:S(2)}) copy-start(s32[14,32]{1,0:T(8,128)} %param.13) | copy-start | bytes 5380
  119.1 212.9 %reduce-scatter.2.cloned.1.call-start = ((), (), s32[]{:S(2)}) async-start(), calls=%async_computation.3 | async-start | bytes 9437184 | tf_op jit(solution)/shard_map/reduce_scatter | solution.py:34
Sparse Core Ops, SparseCore 0:
  9.5 76.0 all-gather.1
  119.2 36.7 all-reduce.1
  181.8 150.1 reduce-scatter.1
where the time goes:
time: 342 us; the launch traced here: 341 us
  waiting for transfers between devices  188 us (55%)
  local copies, waits for them, and re-layouts  61.3 us (18%)
  matrix products  40.9 us (12%)
  other arithmetic  37.2 us (11%)
  between operations  13.1 us (4%)
    reduce_scatter x1, waiting for transfers between devices, body(): lax.psum_scatter(jnp.dot(hidden, down_kept, preferred_element_type=jnp.fl...  150 us
    unnamed x4, local copies, waits for them, and re-layouts  39.9 us
    psum x1, waiting for transfers between devices, body(): summed = lax.psum(partial_sums, 'col')  36.7 us
    mul x1, other arithmetic, expand_mask(): return weight * spread.reshape(weight.shape).astype(weight.dtype)  33.7 us
    dot_general x1, matrix products, body(): jnp.dot(lax.all_gather(tokens, 'row', axis=0, tiled=True), both_kept, pre...  22.5 us
    broadcast_in_dim x3, local copies, waits for them, and re-layouts, expand_mask(): jnp.broadcast_to(mask[:, None, :, None], (blocks_down, side_down, blocks_...  21.5 us
    dot_general x1, matrix products, body(): jnp.dot(hidden, down_kept, preferred_element_type=jnp.float32)  18.4 us
  transfers between devices with their start and end apart: 3, of which 2 were waited for; matrix products, arithmetic and copies ran while one was open for 26% of the time, Pallas kernels for 0%

commit v1 on v0

v1 whole, which is shorter than its diff:
```python
import functools

import jax
import jax.numpy as jnp
from jax import lax
from jax.experimental import pallas as pl
from jax.experimental.pallas import tpu as pltpu
from jax.sharding import PartitionSpec as P

SIDE = 128
UNROLL = 4
SLOTS = 8
CHUNKS = 2
F32 = jnp.float32
BF16 = jnp.bfloat16


def list_kernel(*refs):
    masks, (index, count) = refs[:-2], refs[-2:]
    at = 0
    for mask in masks:
        deep, wide = mask.shape

        def column(j, _, mask=mask, deep=deep, at=at):
            def row(i, n):
                index[at + j, n] = i
                return n + jnp.where(mask[i, j] != 0, 1, 0)

            n = lax.fori_loop(0, deep, row, 0)
            for t in range(UNROLL):
                index[at + j, n + t] = 0
            count[0, at + j] = n
            return 0

        lax.fori_loop(0, wide, column, 0)
        at += wide


def kept_lists(*masks):
    deep = masks[0].shape[0]
    wide = sum(m.shape[1] for m in masks)
    smem = pl.BlockSpec(memory_space=pltpu.SMEM)
    return pl.pallas_call(
        list_kernel,
        out_shape=(
            jax.ShapeDtypeStruct((wide, deep + UNROLL), jnp.int32),
            jax.ShapeDtypeStruct((1, wide), jnp.int32),
        ),
        in_specs=[smem] * len(masks),
        out_specs=(smem, smem),
    )(*masks)


def fetch_column(j, index, count, columns, weights, slots, sems, go):
    slot = lax.rem(j, SLOTS)
    per, first, offset = columns
    for w, weight in enumerate(weights):

        @pl.when(j // per == w)
        def _(w=w, weight=weight):
            here = first + lax.rem(j, per)
            listed = w * offset + here

            def one(t, _):
                i = index[listed, t]
                copy = pltpu.make_async_copy(
                    weight.at[pl.ds(pl.multiple_of(i * SIDE, SIDE), SIDE), pl.ds(pl.multiple_of(here * SIDE, SIDE), SIDE)],
                    slots.at[slot, pl.ds(pl.multiple_of(t * SIDE, SIDE), SIDE), :],
                    sems.at[slot],
                )
                if go:
                    copy.start()
                else:
                    copy.wait()
                return 0

            lax.fori_loop(0, count[0, listed], one, 0)


def multiply_column(j, index, count, columns, held, slots, out):
    slot = lax.rem(j, SLOTS)
    per, first, offset = columns
    listed = (j // per) * offset + first + lax.rem(j, per)
    n = count[0, listed]
    rows = held.shape[0]
    for t in range(UNROLL - 1):
        slots[slot, pl.ds(pl.multiple_of((n + t) * SIDE, SIDE), SIDE), :] = jnp.zeros((SIDE, SIDE), BF16)

    def step(s, total):
        lhs = jnp.concatenate(
            [held[:, pl.ds(pl.multiple_of(index[listed, s * UNROLL + t] * SIDE, SIDE), SIDE)] for t in range(UNROLL)],
            axis=1,
        )
        deep = UNROLL * SIDE
        rhs = slots[slot, pl.ds(pl.multiple_of(s * deep, deep), deep), :]
        return total + jnp.dot(lhs, rhs, preferred_element_type=F32)

    out[...] = lax.fori_loop(0, (n + UNROLL - 1) // UNROLL, step, jnp.zeros((rows, SIDE), F32)).astype(out.dtype)


def gate_up_kernel(columns, places, index, count, *refs):
    pieces = refs[: len(places)]
    gate, up, out, held, slots, sems, piece_sems = refs[len(places) :]
    j = pl.program_id(0)
    wide = pl.num_programs(0)
    fetch = functools.partial(fetch_column, index=index, count=count, columns=columns, weights=(gate, up), slots=slots, sems=sems)
    copies = [
        pltpu.make_async_copy(
            piece, held.at[pl.ds(row, piece.shape[0]), pl.ds(column, piece.shape[1])], piece_sems.at[k]
        )
        for k, (piece, (row, column)) in enumerate(zip(pieces, places))
    ]

    @pl.when(j == 0)
    def _():
        for copy in copies:
            copy.start()
        lax.fori_loop(0, jnp.minimum(SLOTS - 1, wide), lambda k, _: (fetch(k, go=True), 0)[1], 0)
        for copy in copies:
            copy.wait()

    @pl.when(j + SLOTS - 1 < wide)
    def _():
        fetch(j + SLOTS - 1, go=True)

    fetch(j, go=False)
    multiply_column(j, index, count, columns, held, slots, out)


def gate_up(index, count, pieces, places, gate, up, first, blocks):
    deep, width = gate.shape
    rows = max(row + piece.shape[0] for piece, (row, _) in zip(pieces, places))
    wide = 2 * blocks
    return pl.pallas_call(
        functools.partial(gate_up_kernel, (blocks, first, width // SIDE), places),
        out_shape=jax.ShapeDtypeStruct((rows, wide * SIDE), F32),
        grid_spec=pltpu.PrefetchScalarGridSpec(
            num_scalar_prefetch=2,
            grid=(wide,),
            in_specs=[pl.BlockSpec(memory_space=pl.ANY)] * (len(pieces) + 2),
            out_specs=pl.BlockSpec((rows, SIDE), lambda j, *_: (0, j)),
            scratch_shapes=[
                pltpu.VMEM((rows, deep), BF16),
                pltpu.VMEM((SLOTS, deep + (UNROLL - 1) * SIDE, SIDE), BF16),
                pltpu.SemaphoreType.DMA((SLOTS,)),
                pltpu.SemaphoreType.DMA((len(pieces),)),
            ],
        ),
        compiler_params=pltpu.CompilerParams(vmem_limit_bytes=40 << 20),
        cost_estimate=pl.CostEstimate(
            flops=rows * deep * wide * SIDE, bytes_accessed=deep * wide * SIDE, transcendentals=0
        ),
    )(index, count, *pieces, gate, up)


def down_kernel(parts, blocks, index, count, *refs):
    sums = refs[: 2 * parts]
    down, out, held, slots, sems, mine, other, sum_sems = refs[2 * parts :]
    j = pl.program_id(0)
    wide = pl.num_programs(0)
    columns = (wide, 0, 0)
    fetch = functools.partial(fetch_column, index=index, count=count, columns=columns, weights=(down,), slots=slots, sems=sems)

    @pl.when(j == 0)
    def _():
        copies = []
        for k in range(parts):
            copies.append(
                (
                    pltpu.make_async_copy(sums[k], mine.at[k], sum_sems.at[2 * k]),
                    pltpu.make_async_copy(sums[parts + k], other.at[k], sum_sems.at[2 * k + 1]),
                )
            )
        for pair in copies:
            for copy in pair:
                copy.start()
        lax.fori_loop(0, jnp.minimum(SLOTS - 1, wide), lambda k, _: (fetch(k, go=True), 0)[1], 0)
        width = blocks * SIDE
        rows = held.shape[0]
        for k, pair in enumerate(copies):
            for copy in pair:
                copy.wait()

            def some(r, _, k=k):
                at = pl.ds(pl.multiple_of(r * 16, 16), 16)
                gate = mine[k, at, :width] + other[k, at, :width]
                up = mine[k, at, width:] + other[k, at, width:]
                held[at, pl.ds(k * width, width)] = (gate / (1.0 + jnp.exp(-gate)) * up).astype(BF16)
                return 0

            lax.fori_loop(0, rows // 16, some, 0)

    @pl.when(j + SLOTS - 1 < wide)
    def _():
        fetch(j + SLOTS - 1, go=True)

    fetch(j, go=False)
    multiply_column(j, index, count, columns, held, slots, out)


def down_product(index, count, mine, other, down):
    deep, width = down.shape
    parts = len(mine)
    rows, both = mine[0].shape
    wide = width // SIDE
    return pl.pallas_call(
        functools.partial(down_kernel, parts, both // 2 // SIDE),
        out_shape=jax.ShapeDtypeStruct((rows, width), F32),
        grid_spec=pltpu.PrefetchScalarGridSpec(
            num_scalar_prefetch=2,
            grid=(wide,),
            in_specs=[pl.BlockSpec(memory_space=pl.ANY)] * (2 * parts + 1),
            out_specs=pl.BlockSpec((rows, SIDE), lambda j, *_: (0, j)),
            scratch_shapes=[
                pltpu.VMEM((rows, deep), BF16),
                pltpu.VMEM((SLOTS, deep + (UNROLL - 1) * SIDE, SIDE), BF16),
                pltpu.SemaphoreType.DMA((SLOTS,)),
                pltpu.VMEM((parts, rows, both), F32),
                pltpu.VMEM((parts, rows, both), F32),
                pltpu.SemaphoreType.DMA((2 * parts,)),
            ],
        ),
        compiler_params=pltpu.CompilerParams(vmem_limit_bytes=48 << 20),
        cost_estimate=pl.CostEstimate(
            flops=rows * deep * width, bytes_accessed=deep * width, transcendentals=rows * deep
        ),
    )(index, count, *mine, *other, down)


def ring_of(n):
    order = list(range(n)) if n > 8 else list(range(0, n, 2)) + list(range(n - 1, 0, -2))
    onward = [(order[k], order[(k + 1) % n]) for k in range(n)]
    return onward, [(b, a) for a, b in onward]


def gather(block, onward, back, n):
    behind, ahead = [block], [block]
    for _ in range(n // 2 - 1):
        behind.append(lax.ppermute(behind[-1], "row", onward))
        ahead.append(lax.ppermute(ahead[-1], "row", back))
    half = block.shape[1] // 2
    left = lax.ppermute(behind[-1][:, :half], "row", onward)
    right = lax.ppermute(ahead[-1][:, half:], "row", back)
    return behind + ahead[1:], (left, right)


def scatter(part, rows, onward, back, n):
    half = part.shape[1] // 2
    far = n // 2

    def block(k):
        at = 0 if k == 0 else (n - 1 if abs(k) == far else (-k if k < 0 else far - 1 + k))
        return part[at * rows : (at + 1) * rows]

    on = lax.ppermute(block(far)[:, :half].astype(BF16), "row", onward)
    ba = lax.ppermute(block(far)[:, half:].astype(BF16), "row", back)
    for k in range(far - 1, 0, -1):
        if k == far - 1:
            on_sum = jnp.concatenate((block(k)[:, :half] + on.astype(F32), block(k)[:, half:]), axis=1)
            ba_sum = jnp.concatenate((block(-k)[:, :half], block(-k)[:, half:] + ba.astype(F32)), axis=1)
        else:
            on_sum = block(k) + on.astype(F32)
            ba_sum = block(-k) + ba.astype(F32)
        on = lax.ppermute(on_sum.astype(BF16), "row", onward)
        ba = lax.ppermute(ba_sum.astype(BF16), "row", back)
    return (block(0) + on.astype(F32) + ba.astype(F32)).astype(BF16)


def body(n, tokens, gate, up, down, gate_mask, up_mask, down_mask):
    onward, back = ring_of(n)
    swap = [(0, 1), (1, 0)]
    rows = tokens.shape[0] // CHUNKS
    half = tokens.shape[1] // 2
    hidden_blocks = gate.shape[1] // SIDE
    index, count = kept_lists(gate_mask, up_mask)
    down_index, down_count = kept_lists(down_mask)

    cut = (hidden_blocks + 1) // 2
    spans = ((0, hidden_blocks),)
    outs = []
    for c in range(CHUNKS):
        blocks, (left, right) = gather(tokens[c * rows : (c + 1) * rows], onward, back, n)
        pieces = blocks + [left, right]
        places = [(k * rows, 0) for k in range(n - 1)] + [((n - 1) * rows, 0), ((n - 1) * rows, half)]
        mine = [gate_up(index, count, pieces, places, gate, up, first, some) for first, some in spans]
        other = [lax.ppermute(m, "col", swap) for m in mine]
        part = down_product(down_index, down_count, mine, other, down)
        outs.append(scatter(part, rows, onward, back, n))
    return jnp.concatenate(outs, axis=0)


def solution(mesh):
    return jax.shard_map(
        functools.partial(body, mesh.shape["row"]),
        mesh=mesh,
        in_specs=(
            P(("groups", "row"), "col"),
            P("col", "row"),
            P("col", "row"),
            P("row", "col"),
            P("col", "row"),
            P("col", "row"),
            P("row", "col"),
        ),
        out_specs=P(("groups", "row"), "col"),
        check_vma=False,
    )
```

time: 342 us -> 220 us (0.64)
  waiting for transfers between devices: 188 us -> 56.6 us
  Pallas kernels: 0 us -> 104 us
  local copies, waits for them, and re-layouts: 61.3 us -> 7.25 us
  starting transfers between devices: 0.26 us -> 47.3 us
  matrix products: 40.9 us -> 0 us
  other arithmetic: 37.2 us -> 6.7 us
  between operations: 13.1 us -> 0.3 us
    reduce_scatter x1 -> x0, waiting for transfers between devices: 150 us -> none  [body(): lax.psum_scatter(jnp.dot(hidden, down_kept, preferred_element_type=jnp.fl...]
    pallas_call x0 -> x6, Pallas kernels: none -> 104 us  [the longest x2 43.9 us: gate_up(): pl.pallas_call(functools.partial(gate_up_kernel, (blocks, first, width //...]
    ppermute x0 -> x34, waiting for transfers between devices: none -> 56.6 us  [the longest x6 18.6 us: gather(): behind.append(lax.ppermute(behind[-1], 'row', onward))]
    ppermute x0 -> x34, starting transfers between devices: none -> 47.3 us  [the longest x6 12.2 us: scatter(): ba = lax.ppermute(ba_sum.astype(BF16), 'row', back)]
    dot_general x2 -> x0, matrix products: 40.9 us -> none  [the longest x1 22.5 us: body(): jnp.dot(lax.all_gather(tokens, 'row', axis=0, tiled=True), both_kept, pre...]
    psum x1 -> x0, waiting for transfers between devices: 36.7 us -> none  [body(): summed = lax.psum(partial_sums, 'col')]
    unnamed x4 -> x14, local copies, waits for them, and re-layouts: 39.9 us -> 5.41 us
    mul x1 -> x0, other arithmetic: 33.7 us -> none  [expand_mask(): return weight * spread.reshape(weight.shape).astype(weight.dtype)]
  transfers between devices with their start and end apart: 3 -> 34, of which waited for: 2 -> 14; matrix products, arithmetic and copies ran while one was open for 26% -> 4% of each run, Pallas kernels for 0% -> 47%
where the time goes in v1:
time: 220 us; the launch traced here: 222 us
  Pallas kernels  104 us (47%)
  waiting for transfers between devices  56.6 us (26%)
  starting transfers between devices  47.3 us (22%)
  local copies, waits for them, and re-layouts  7.25 us (3%)
  other arithmetic  6.7 us (3%)
    pallas_call x2, Pallas kernels, gate_up(): pl.pallas_call(functools.partial(gate_up_kernel, (blocks, first, width //...  43.9 us
    pallas_call x2, Pallas kernels, down_product(): pl.pallas_call(functools.partial(down_kernel, parts, both // 2 // SIDE),...  41.8 us
    ppermute x6, waiting for transfers between devices, gather(): behind.append(lax.ppermute(behind[-1], 'row', onward))  18.6 us
    pallas_call x2, Pallas kernels, kept_lists(): pl.pallas_call(list_kernel, out_shape=(jax.ShapeDtypeStruct((wide, deep +...  18.1 us
    ppermute x6, waiting for transfers between devices, scatter(): on = lax.ppermute(on_sum.astype(BF16), 'row', onward)  15.3 us
    ppermute x6, starting transfers between devices, scatter(): ba = lax.ppermute(ba_sum.astype(BF16), 'row', back)  12.2 us
    ppermute x6, starting transfers between devices, gather(): behind.append(lax.ppermute(behind[-1], 'row', onward))  12.1 us
    ppermute x6, waiting for transfers between devices, scatter(): ba = lax.ppermute(ba_sum.astype(BF16), 'row', back)  11.3 us
  transfers between devices with their start and end apart: 34, of which 14 were waited for; matrix products, arithmetic and copies ran while one was open for 4% of the time, Pallas kernels for 47%

profile of v1, /device:TPU:0, one launch (start us, length us, event | category | flops | bytes accessed | tf_op | source)
XLA Modules:
  0.0 221.9 jit_solution(15827694711741666025)
XLA Ops:
  0.0 1.1 fusion.18
  1.1 3.1 %collective-permute-start = (bf16[32,4096]{1,0:T(8,128)(2,1)S(1)}, bf16[32,4096]{1,0:T(8,128)(2,1)S(1)}, u32[]{:S(2)}, u32[]{:S(2)}) collective-permute-start(bf16[32,4096]{1,0:T(8,128)(2,1)S(1)} %get-tuple-element.29.refs_0_), channel_id=1, source_target_pairs={{0,4},{4,8},{8,12},{12,14},{14,10},{10,6},{6,2},{2,0},{1,5},{5,9},... | collective-permute-start | bytes 786440 | tf_op jit(solution)/shard_map/ppermute | solution.py:239
  4.2 6.2 %collective-permute-done.refs_1_ = bf16[32,4096]{1,0:T(8,128)(2,1)S(1)} collective-permute-done((bf16[32,4096]{1,0:T(8,128)(2,1)S(1)}, bf16[32,4096]{1,0:T(8,128)(2,1)S(1)}, u32[]{:S(2)}, u32[]{:S(2)}) %collective-permute-start) | collective-permute-done | bytes 262176 | tf_op jit(solution)/shard_map/ppermute | solution.py:239
  10.4 1.8 collective-permute-start.1
  12.2 0.2 collective-permute-start.4
  12.4 1.8 collective-permute-start.17
  14.2 0.2 collective-permute-start.20
  14.4 5.2 %collective-permute-done.1.refs_2_ = bf16[32,4096]{1,0:T(8,128)(2,1)S(1)} collective-permute-done((bf16[32,4096]{1,0:T(8,128)(2,1)S(1)}, bf16[32,4096]{1,0:T(8,128)(2,1)S(1)}, u32[]{:S(2)}, u32[]{:S(2)}) %collective-permute-start.1) | collective-permute-done | bytes 262176 | tf_op jit(solution)/shard_map/ppermute | solution.py:239
  19.6 1.8 collective-permute-start.2
  21.4 0.2 collective-permute-start.5
  21.7 3.6 %collective-permute-done.17.refs_1_ = bf16[32,4096]{1,0:T(8,128)(2,1)S(1)} collective-permute-done((bf16[32,4096]{1,0:T(8,128)(2,1)S(1)}, bf16[32,4096]{1,0:T(8,128)(2,1)S(1)}, u32[]{:S(2)}, u32[]{:S(2)}) %collective-permute-start.17) | collective-permute-done | bytes 262176 | tf_op jit(solution)/shard_map/ppermute | solution.py:239
  25.3 1.8 collective-permute-start.18
  27.1 0.2 collective-permute-start.21
  27.3 3.6 %collective-permute-done.2.refs_3_ = bf16[32,4096]{1,0:T(8,128)(2,1)S(1)} collective-permute-done((bf16[32,4096]{1,0:T(8,128)(2,1)S(1)}, bf16[32,4096]{1,0:T(8,128)(2,1)S(1)}, u32[]{:S(2)}, u32[]{:S(2)}) %collective-permute-start.2) | collective-permute-done | bytes 262176 | tf_op jit(solution)/shard_map/ppermute | solution.py:239
  30.9 1.8 collective-permute-start.6
  32.7 0.7 slice.145
  33.4 0.2 collective-permute-start.7
  33.6 1.4 copy.8.refs_0_
  35.0 1.4 copy.9.refs_1_
  36.4 11.6 %shard_map.74 = (s32[28,36]{1,0:T(8,128)}, s32[1,28]{1,0:T(1,128)}) custom-call(s32[32,14]{1,0:T(8,128)} %copy.8.refs_0_, s32[32,14]{1,0:T(8,128)} %copy.9.refs_1_), custom_call_target="tpu_custom_call" | custom-call | tf_op jit(solution)/shard_map/pallas_call | solution.py:43
  48.0 1.8 collective-permute-start.19
  49.8 0.2 collective-permute-start.22
  50.1 0.7 copy-done
  50.8 0.6 copy-done.3
  51.4 22.0 %shard_map.75.refs_0_ = f32[256,3584]{1,0:T(8,128)} custom-call(s32[28,36]{1,0:T(8,128)S(1)} %copy-done, s32[1,28]{1,0:T(1,128)S(1)} %copy-done.3, bf16[32,4096]{1,0:T(8,128)(2,1)S(1)} %get-tuple-element.29.refs_0_, bf16[32,4096]{1,0:T(8,128)(2,1)S(1)} %collective-permute-done.refs_1_, bf16[32,4096]{1,0:T(8,128)(2,1)S(1)} %collective-permute-done.1.refs_2_, ...), custom_call_target="tpu_custom_call" | custom-call | flops 3758096384 | bytes 14680064 | tf_op jit(solution)/shard_map/pallas_call | solution.py:134
  73.4 0.1 collective-permute-start.8
  73.5 3.8 %collective-permute-start.23 = (bf16[32,2048]{1,0:T(8,128)(2,1)S(1)}, bf16[32,2048]{1,0:T(8,128)(2,1)S(1)}, u32[]{:S(2)}, u32[]{:S(2)}) collective-permute-start(bf16[32,2048]{1,0:T(8,128)(2,1)S(1)} %slice.157), channel_id=1, source_target_pairs={{0,4},{4,8},{8,12},{12,14},{14,10},{10,6},{6,2},{2,0},{1,5},{5,9},... | collective-permute-start | bytes 393224 | tf_op jit(solution)/shard_map/ppermute | solution.py:242
  77.4 3.3 %collective-permute-done.23.refs_7_ = bf16[32,2048]{1,0:T(8,128)(2,1)S(1)} collective-permute-done((bf16[32,2048]{1,0:T(8,128)(2,1)S(1)}, bf16[32,2048]{1,0:T(8,128)(2,1)S(1)}, u32[]{:S(2)}, u32[]{:S(2)}) %collective-permute-start.23) | collective-permute-done | bytes 131104 | tf_op jit(solution)/shard_map/ppermute | solution.py:242
  80.8 4.0 %collective-permute-done.24.refs_8_ = bf16[32,2048]{1,0:T(8,128)(2,1)S(1)} collective-permute-done((bf16[32,2048]{1,0:T(8,128)(2,1)S(1)}, bf16[32,2048]{1,0:T(8,128)(2,1)S(1)}, u32[]{:S(2)}, u32[]{:S(2)}) %collective-permute-start.24) | collective-permute-done | bytes 131104 | tf_op jit(solution)/shard_map/ppermute | solution.py:243
  84.8 21.9 %shard_map.77.refs_0_ = f32[256,3584]{1,0:T(8,128)} custom-call(s32[28,36]{1,0:T(8,128)S(1)} %copy-done, s32[1,28]{1,0:T(1,128)S(1)} %copy-done.3, bf16[32,4096]{1,0:T(8,128)(2,1)S(1)} %get-tuple-element.30.refs_0_, bf16[32,4096]{1,0:T(8,128)(2,1)S(1)} %collective-permute-done.17.refs_1_, bf16[32,4096]{1,0:T(8,128)(2,1)S(1)} %collective-permute-done.18.refs_2_, ...), custom_call_target="tpu_custom_call" | custom-call | flops 3758096384 | bytes 14680064 | tf_op jit(solution)/shard_map/pallas_call | solution.py:134
  106.7 1.4 collective-permute-start.25
  108.1 6.5 %shard_map.73 = (s32[32,18]{1,0:T(8,128)}, s32[1,32]{1,0:T(1,128)}) custom-call(s32[14,32]{1,0:T(8,128)} %refs_0_.2), custom_call_target="tpu_custom_call" | custom-call | tf_op jit(solution)/shard_map/pallas_call | solution.py:43
  114.6 0.7 copy-done.1
  115.4 0.6 copy-done.2
  116.0 20.9 %shard_map.76 = f32[256,4096]{1,0:T(8,128)} custom-call(s32[32,18]{1,0:T(8,128)S(1)} %copy-done.1, s32[1,32]{1,0:T(1,128)S(1)} %copy-done.2, f32[256,3584]{1,0:T(8,128)} %shard_map.75.refs_0_, f32[256,3584]{1,0:T(8,128)} %collective-permute-done.8.refs_1_, bf16[1792,4096]{1,0:T(8,128)(2,1)} %refs_2_.3), custom_call_target="tpu_custom_call" | custom-call | flops 1879048192 | bytes 7340032 | tf_op jit(solution)/shard_map/pallas_call | solution.py:206
  136.9 2.5 %convert.28 = bf16[256,4096]{1,0:T(8,128)(2,1)S(1)} convert(f32[256,4096]{1,0:T(8,128)} %shard_map.76) | non-fusion elementwise | flops 1048576 | bytes 6291456 | tf_op jit(solution)/shard_map/convert.15
  139.4 4.7 %collective-permute-start.9 = (bf16[32,2048]{1,0:T(8,128)(2,1)S(1)}, bf16[32,2048]{1,0:T(8,128)(2,1)S(1)}, u32[]{:S(2)}, u32[]{:S(2)}) collective-permute-start(bf16[32,2048]{1,0:T(8,128)(2,1)S(1)} %get-tuple-element.21), channel_id=1, source_target_pairs={{0,4},{4,8},{8,12},{12,14},{14,10},{10,6},{6,2},{2,0},{1,5},{5,9},... | collective-permute-start | bytes 393224 | tf_op jit(solution)/shard_map/ppermute | solution.py:255
  144.1 20.9 %shard_map.78 = f32[256,4096]{1,0:T(8,128)} custom-call(s32[32,18]{1,0:T(8,128)S(1)} %copy-done.1, s32[1,32]{1,0:T(1,128)S(1)} %copy-done.2, f32[256,3584]{1,0:T(8,128)} %shard_map.77.refs_0_, f32[256,3584]{1,0:T(8,128)} %collective-permute-done.25.refs_1_, bf16[1792,4096]{1,0:T(8,128)(2,1)} %refs_2_.3), custom_call_target="tpu_custom_call" | custom-call | flops 1879048192 | bytes 7340032 | tf_op jit(solution)/shard_map/pallas_call | solution.py:206
  165.0 2.6 %convert.31 = bf16[256,4096]{1,0:T(8,128)(2,1)S(1)} convert(f32[256,4096]{1,0:T(8,128)} %shard_map.78) | non-fusion elementwise | flops 1048576 | bytes 6291456 | tf_op jit(solution)/shard_map/convert.7
  167.7 4.7 %collective-permute-start.26 = (bf16[32,2048]{1,0:T(8,128)(2,1)S(1)}, bf16[32,2048]{1,0:T(8,128)(2,1)S(1)}, u32[]{:S(2)}, u32[]{:S(2)}) collective-permute-start(bf16[32,2048]{1,0:T(8,128)(2,1)S(1)} %get-tuple-element.25), channel_id=1, source_target_pairs={{0,4},{4,8},{8,12},{12,14},{14,10},{10,6},{6,2},{2,0},{1,5},{5,9},... | collective-permute-start | bytes 393224 | tf_op jit(solution)/shard_map/ppermute | solution.py:255
  172.5 0.6 collective-permute-start.30
  173.0 0.1 fusion.15
  173.1 4.0 %collective-permute-start.14 = (bf16[32,4096]{1,0:T(8,128)(2,1)S(1)}, bf16[32,4096]{1,0:T(8,128)(2,1)S(1)}, u32[]{:S(2)}, u32[]{:S(2)}) collective-permute-start(bf16[32,4096]{1,0:T(8,128)(2,1)S(1)} %pad_maximum_fusion.2), channel_id=1, source_target_pairs={{4,0},{8,4},{12,8},{14,12},{10,14},{6,10},{2,6},{0,2},{5,1},{9,5},... | collective-permute-start | bytes 786440 | tf_op jit(solution)/shard_map/ppermute | solution.py:265
  177.2 4.0 %collective-permute-done.30 = bf16[32,2048]{1,0:T(8,128)(2,1)S(1)} collective-permute-done((bf16[32,2048]{1,0:T(8,128)(2,1)S(1)}, bf16[32,2048]{1,0:T(8,128)(2,1)S(1)}, u32[]{:S(2)}, u32[]{:S(2)}) %collective-permute-start.30) | collective-permute-done | bytes 131104 | tf_op jit(solution)/shard_map/ppermute | solution.py:256
  181.2 0.1 fusion.13
  181.4 2.7 %collective-permute-start.27 = (bf16[32,4096]{1,0:T(8,128)(2,1)S(1)}, bf16[32,4096]{1,0:T(8,128)(2,1)S(1)}, u32[]{:S(2)}, u32[]{:S(2)}) collective-permute-start(bf16[32,4096]{1,0:T(8,128)(2,1)S(1)} %pad_maximum_fusion.3), channel_id=1, source_target_pairs={{0,4},{4,8},{8,12},{12,14},{14,10},{10,6},{6,2},{2,0},{1,5},{5,9},... | collective-permute-start | bytes 786440 | tf_op jit(solution)/shard_map/ppermute | solution.py:264
  184.1 2.3 %collective-permute-done.10 = bf16[32,4096]{1,0:T(8,128)(2,1)S(1)} collective-permute-done((bf16[32,4096]{1,0:T(8,128)(2,1)S(1)}, bf16[32,4096]{1,0:T(8,128)(2,1)S(1)}, u32[]{:S(2)}, u32[]{:S(2)}) %collective-permute-start.10) | collective-permute-done | bytes 262176 | tf_op jit(solution)/shard_map/ppermute | solution.py:264
  186.4 0.1 collective-permute-start.11
  186.5 5.4 %collective-permute-done.27 = bf16[32,4096]{1,0:T(8,128)(2,1)S(1)} collective-permute-done((bf16[32,4096]{1,0:T(8,128)(2,1)S(1)}, bf16[32,4096]{1,0:T(8,128)(2,1)S(1)}, u32[]{:S(2)}, u32[]{:S(2)}) %collective-permute-start.27) | collective-permute-done | bytes 262176 | tf_op jit(solution)/shard_map/ppermute | solution.py:264
  192.0 1.4 collective-permute-start.28
  193.4 4.2 %collective-permute-done.11 = bf16[32,4096]{1,0:T(8,128)(2,1)S(1)} collective-permute-done((bf16[32,4096]{1,0:T(8,128)(2,1)S(1)}, bf16[32,4096]{1,0:T(8,128)(2,1)S(1)}, u32[]{:S(2)}, u32[]{:S(2)}) %collective-permute-start.11) | collective-permute-done | bytes 262176 | tf_op jit(solution)/shard_map/ppermute | solution.py:264
  197.6 0.1 fusion.9
  197.7 2.1 collective-permute-start.15
  199.8 3.4 %collective-permute-done.28 = bf16[32,4096]{1,0:T(8,128)(2,1)S(1)} collective-permute-done((bf16[32,4096]{1,0:T(8,128)(2,1)S(1)}, bf16[32,4096]{1,0:T(8,128)(2,1)S(1)}, u32[]{:S(2)}, u32[]{:S(2)}) %collective-permute-start.28) | collective-permute-done | bytes 262176 | tf_op jit(solution)/shard_map/ppermute | solution.py:264
  203.2 0.1 fusion.3
  203.3 2.1 collective-permute-start.32
  205.4 2.1 collective-permute-start.16
  207.5 5.1 %collective-permute-done.32 = bf16[32,4096]{1,0:T(8,128)(2,1)S(1)} collective-permute-done((bf16[32,4096]{1,0:T(8,128)(2,1)S(1)}, bf16[32,4096]{1,0:T(8,128)(2,1)S(1)}, u32[]{:S(2)}, u32[]{:S(2)}) %collective-permute-start.32) | collective-permute-done | bytes 262176 | tf_op jit(solution)/shard_map/ppermute | solution.py:265
  212.7 2.1 collective-permute-start.33
  214.7 3.4 %collective-permute-done.16 = bf16[32,4096]{1,0:T(8,128)(2,1)S(1)} collective-permute-done((bf16[32,4096]{1,0:T(8,128)(2,1)S(1)}, bf16[32,4096]{1,0:T(8,128)(2,1)S(1)}, u32[]{:S(2)}, u32[]{:S(2)}) %collective-permute-start.16) | collective-permute-done | bytes 262176 | tf_op jit(solution)/shard_map/ppermute | solution.py:265
  218.1 0.1 fusion.11
  218.3 2.7 %collective-permute-done.33 = bf16[32,4096]{1,0:T(8,128)(2,1)S(1)} collective-permute-done((bf16[32,4096]{1,0:T(8,128)(2,1)S(1)}, bf16[32,4096]{1,0:T(8,128)(2,1)S(1)}, u32[]{:S(2)}, u32[]{:S(2)}) %collective-permute-start.33) | collective-permute-done | bytes 262176 | tf_op jit(solution)/shard_map/ppermute | solution.py:265
  221.0 0.1 fusion.5
  221.1 0.8 pad_maximum_fusion
  (48 shorter events, 0.8 us)
Async XLA Ops:
  1.1 9.3 %collective-permute-start = (bf16[32,4096]{1,0:T(8,128)(2,1)S(1)}, bf16[32,4096]{1,0:T(8,128)(2,1)S(1)}, u32[]{:S(2)}, u32[]{:S(2)}) collective-permute-start(bf16[32,4096]{1,0:T(8,128)(2,1)S(1)} %get-tuple-element.29.refs_0_), channel_id=1, source_target_pairs={{0,4},{4,8},{8,12},{12,14},{14,10},{10,6},{6,2},{2,0},{1,5},{5,9},... | collective-permute-start | bytes 786440 | tf_op jit(solution)/shard_map/ppermute | solution.py:239
  4.1 8.0 %collective-permute-start.3 = (bf16[32,4096]{1,0:T(8,128)(2,1)S(1)}, bf16[32,4096]{1,0:T(8,128)(2,1)S(1)}, u32[]{:S(2)}, u32[]{:S(2)}) collective-permute-start(bf16[32,4096]{1,0:T(8,128)(2,1)S(1)} %get-tuple-element.29.refs_0_), channel_id=1, source_target_pairs={{4,0},{8,4},{12,8},{14,12},{10,14},{6,10},{2,6},{0,2},{5,1},{9,5},... | collective-permute-start | bytes 786440 | tf_op jit(solution)/shard_map/ppermute | solution.py:240
  10.4 9.2 %collective-permute-start.1 = (bf16[32,4096]{1,0:T(8,128)(2,1)S(1)}, bf16[32,4096]{1,0:T(8,128)(2,1)S(1)}, u32[]{:S(2)}, u32[]{:S(2)}) collective-permute-start(bf16[32,4096]{1,0:T(8,128)(2,1)S(1)} %collective-permute-done.refs_1_), channel_id=1, source_target_pairs={{0,4},{4,8},{8,12},{12,14},{14,10},{10,6},{6,2},{2,0},{1,5},{5,9},... | collective-permute-start | bytes 786440 | tf_op jit(solution)/shard_map/ppermute | solution.py:239
  12.2 9.2 %collective-permute-start.4 = (bf16[32,4096]{1,0:T(8,128)(2,1)S(1)}, bf16[32,4096]{1,0:T(8,128)(2,1)S(1)}, u32[]{:S(2)}, u32[]{:S(2)}) collective-permute-start(bf16[32,4096]{1,0:T(8,128)(2,1)S(1)} %collective-permute-done.3.refs_4_), channel_id=1, source_target_pairs={{4,0},{8,4},{12,8},{14,12},{10,14},{6,10},{2,6},{0,2},{5,1},{9,5},... | collective-permute-start | bytes 786440 | tf_op jit(solution)/shard_map/ppermute | solution.py:240
  12.4 12.8 %collective-permute-start.17 = (bf16[32,4096]{1,0:T(8,128)(2,1)S(1)}, bf16[32,4096]{1,0:T(8,128)(2,1)S(1)}, u32[]{:S(2)}, u32[]{:S(2)}) collective-permute-start(bf16[32,4096]{1,0:T(8,128)(2,1)S(1)} %get-tuple-element.30.refs_0_), channel_id=1, source_target_pairs={{0,4},{4,8},{8,12},{12,14},{14,10},{10,6},{6,2},{2,0},{1,5},{5,9},... | collective-permute-start | bytes 786440 | tf_op jit(solution)/shard_map/ppermute | solution.py:239
  14.2 12.8 %collective-permute-start.20 = (bf16[32,4096]{1,0:T(8,128)(2,1)S(1)}, bf16[32,4096]{1,0:T(8,128)(2,1)S(1)}, u32[]{:S(2)}, u32[]{:S(2)}) collective-permute-start(bf16[32,4096]{1,0:T(8,128)(2,1)S(1)} %get-tuple-element.30.refs_0_), channel_id=1, source_target_pairs={{4,0},{8,4},{12,8},{14,12},{10,14},{6,10},{2,6},{0,2},{5,1},{9,5},... | collective-permute-start | bytes 786440 | tf_op jit(solution)/shard_map/ppermute | solution.py:240
  19.6 11.2 %collective-permute-start.2 = (bf16[32,4096]{1,0:T(8,128)(2,1)S(1)}, bf16[32,4096]{1,0:T(8,128)(2,1)S(1)}, u32[]{:S(2)}, u32[]{:S(2)}) collective-permute-start(bf16[32,4096]{1,0:T(8,128)(2,1)S(1)} %collective-permute-done.1.refs_2_), channel_id=1, source_target_pairs={{0,4},{4,8},{8,12},{12,14},{14,10},{10,6},{6,2},{2,0},{1,5},{5,9},... | collective-permute-start | bytes 786440 | tf_op jit(solution)/shard_map/ppermute | solution.py:239
  21.4 11.3 %collective-permute-start.5 = (bf16[32,4096]{1,0:T(8,128)(2,1)S(1)}, bf16[32,4096]{1,0:T(8,128)(2,1)S(1)}, u32[]{:S(2)}, u32[]{:S(2)}) collective-permute-start(bf16[32,4096]{1,0:T(8,128)(2,1)S(1)} %collective-permute-done.4.refs_5_), channel_id=1, source_target_pairs={{4,0},{8,4},{12,8},{14,12},{10,14},{6,10},{2,6},{0,2},{5,1},{9,5},... | collective-permute-start | bytes 786440 | tf_op jit(solution)/shard_map/ppermute | solution.py:240
  25.3 22.7 %collective-permute-start.18 = (bf16[32,4096]{1,0:T(8,128)(2,1)S(1)}, bf16[32,4096]{1,0:T(8,128)(2,1)S(1)}, u32[]{:S(2)}, u32[]{:S(2)}) collective-permute-start(bf16[32,4096]{1,0:T(8,128)(2,1)S(1)} %collective-permute-done.17.refs_1_), channel_id=1, source_target_pairs={{0,4},{4,8},{8,12},{12,14},{14,10},{10,6},{6,2},{2,0},{1,5},{5,9},... | collective-permute-start | bytes 786440 | tf_op jit(solution)/shard_map/ppermute | solution.py:239
  27.1 22.8 %collective-permute-start.21 = (bf16[32,4096]{1,0:T(8,128)(2,1)S(1)}, bf16[32,4096]{1,0:T(8,128)(2,1)S(1)}, u32[]{:S(2)}, u32[]{:S(2)}) collective-permute-start(bf16[32,4096]{1,0:T(8,128)(2,1)S(1)} %collective-permute-done.20.refs_4_), channel_id=1, source_target_pairs={{4,0},{8,4},{12,8},{14,12},{10,14},{6,10},{2,6},{0,2},{5,1},{9,5},... | collective-permute-start | bytes 786440 | tf_op jit(solution)/shard_map/ppermute | solution.py:240
  30.9 19.2 %collective-permute-start.6 = (bf16[32,2048]{1,0:T(8,128)(2,1)S(1)}, bf16[32,2048]{1,0:T(8,128)(2,1)S(1)}, u32[]{:S(2)}, u32[]{:S(2)}) collective-permute-start(bf16[32,2048]{1,0:T(8,128)(2,1)S(1)} %slice.144), channel_id=1, source_target_pairs={{0,4},{4,8},{8,12},{12,14},{14,10},{10,6},{6,2},{2,0},{1,5},{5,9},... | collective-permute-start | bytes 393224 | tf_op jit(solution)/shard_map/ppermute | solution.py:242
  33.4 16.7 %collective-permute-start.7 = (bf16[32,2048]{1,0:T(8,128)(2,1)}, bf16[32,2048]{1,0:T(8,128)(2,1)S(1)}, u32[]{:S(2)}, u32[]{:S(2)}) collective-permute-start(bf16[32,2048]{1,0:T(8,128)(2,1)} %slice.145), channel_id=1, source_target_pairs={{4,0},{8,4},{12,8},{14,12},{10,14},{6,10},{2,6},{0,2},{5,1},{9,5},... | collective-permute-start | bytes 393224 | tf_op jit(solution)/shard_map/ppermute | solution.py:243
  48.0 25.5 %collective-permute-start.19 = (bf16[32,4096]{1,0:T(8,128)(2,1)S(1)}, bf16[32,4096]{1,0:T(8,128)(2,1)S(1)}, u32[]{:S(2)}, u32[]{:S(2)}) collective-permute-start(bf16[32,4096]{1,0:T(8,128)(2,1)S(1)} %collective-permute-done.18.refs_2_), channel_id=1, source_target_pairs={{0,4},{4,8},{8,12},{12,14},{14,10},{10,6},{6,2},{2,0},{1,5},{5,9},... | collective-permute-start | bytes 786440 | tf_op jit(solution)/shard_map/ppermute | solution.py:239
  49.8 27.5 %collective-permute-start.22 = (bf16[32,4096]{1,0:T(8,128)(2,1)S(1)}, bf16[32,4096]{1,0:T(8,128)(2,1)S(1)}, u32[]{:S(2)}, u32[]{:S(2)}) collective-permute-start(bf16[32,4096]{1,0:T(8,128)(2,1)S(1)} %collective-permute-done.21.refs_5_), channel_id=1, source_target_pairs={{4,0},{8,4},{12,8},{14,12},{10,14},{6,10},{2,6},{0,2},{5,1},{9,5},... | collective-permute-start | bytes 786440 | tf_op jit(solution)/shard_map/ppermute | solution.py:240
  50.1 0.7 copy-start
  50.8 0.6 copy-start.3
  73.4 41.2 %collective-permute-start.8 = (f32[256,3584]{1,0:T(8,128)}, f32[256,3584]{1,0:T(8,128)}, u32[]{:S(2)}, u32[]{:S(2)}) collective-permute-start(f32[256,3584]{1,0:T(8,128)} %shard_map.75.refs_0_), channel_id=1, source_target_pairs={{0,1},{1,0},{2,3},{3,2},{4,5},{5,4},{6,7},{7,6},{8,9},{9,8},{10,11... | collective-permute-start | bytes 11010056 | tf_op jit(solution)/shard_map/ppermute | solution.py:286
  73.5 7.2 %collective-permute-start.23 = (bf16[32,2048]{1,0:T(8,128)(2,1)S(1)}, bf16[32,2048]{1,0:T(8,128)(2,1)S(1)}, u32[]{:S(2)}, u32[]{:S(2)}) collective-permute-start(bf16[32,2048]{1,0:T(8,128)(2,1)S(1)} %slice.157), channel_id=1, source_target_pairs={{0,4},{4,8},{8,12},{12,14},{14,10},{10,6},{6,2},{2,0},{1,5},{5,9},... | collective-permute-start | bytes 393224 | tf_op jit(solution)/shard_map/ppermute | solution.py:242
  77.4 7.4 %collective-permute-start.24 = (bf16[32,2048]{1,0:T(8,128)(2,1)S(1)}, bf16[32,2048]{1,0:T(8,128)(2,1)S(1)}, u32[]{:S(2)}, u32[]{:S(2)}) collective-permute-start(bf16[32,2048]{1,0:T(8,128)(2,1)S(1)} %slice.158), channel_id=1, source_target_pairs={{4,0},{8,4},{12,8},{14,12},{10,14},{6,10},{2,6},{0,2},{5,1},{9,5},... | collective-permute-start | bytes 393224 | tf_op jit(solution)/shard_map/ppermute | solution.py:243
  106.7 37.4 %collective-permute-start.25 = (f32[256,3584]{1,0:T(8,128)}, f32[256,3584]{1,0:T(8,128)}, u32[]{:S(2)}, u32[]{:S(2)}) collective-permute-start(f32[256,3584]{1,0:T(8,128)} %shard_map.77.refs_0_), channel_id=1, source_target_pairs={{0,1},{1,0},{2,3},{3,2},{4,5},{5,4},{6,7},{7,6},{8,9},{9,8},{10,11... | collective-permute-start | bytes 11010056 | tf_op jit(solution)/shard_map/ppermute | solution.py:286
  114.6 0.7 copy-start.1
  115.4 0.6 copy-start.2
  139.4 33.6 %collective-permute-start.13 = (bf16[32,2048]{1,0:T(8,128)(2,1)S(1)}, bf16[32,2048]{1,0:T(8,128)(2,1)S(1)}, u32[]{:S(2)}, u32[]{:S(2)}) collective-permute-start(bf16[32,2048]{1,0:T(8,128)(2,1)S(1)} %get-tuple-element.22), channel_id=1, source_target_pairs={{4,0},{8,4},{12,8},{14,12},{10,14},{6,10},{2,6},{0,2},{5,1},{9,5},... | collective-permute-start | bytes 393224 | tf_op jit(solution)/shard_map/ppermute | solution.py:256
  139.4 33.6 %collective-permute-start.9 = (bf16[32,2048]{1,0:T(8,128)(2,1)S(1)}, bf16[32,2048]{1,0:T(8,128)(2,1)S(1)}, u32[]{:S(2)}, u32[]{:S(2)}) collective-permute-start(bf16[32,2048]{1,0:T(8,128)(2,1)S(1)} %get-tuple-element.21), channel_id=1, source_target_pairs={{0,4},{4,8},{8,12},{12,14},{14,10},{10,6},{6,2},{2,0},{1,5},{5,9},... | collective-permute-start | bytes 393224 | tf_op jit(solution)/shard_map/ppermute | solution.py:255
  165.0 8.0 %copy-start.4 = (f32[256,4096]{1,0:T(8,128)S(1)}, f32[256,4096]{1,0:T(8,128)}, u32[]{:S(2)}) copy-start(f32[256,4096]{1,0:T(8,128)} %shard_map.76) | copy-start | bytes 12582916
  165.0 16.2 %copy-start.5 = (f32[256,4096]{1,0:T(8,128)S(1)}, f32[256,4096]{1,0:T(8,128)}, u32[]{:S(2)}) copy-start(f32[256,4096]{1,0:T(8,128)} %shard_map.78) | copy-start | bytes 12582916
  167.7 9.5 %collective-permute-start.26 = (bf16[32,2048]{1,0:T(8,128)(2,1)S(1)}, bf16[32,2048]{1,0:T(8,128)(2,1)S(1)}, u32[]{:S(2)}, u32[]{:S(2)}) collective-permute-start(bf16[32,2048]{1,0:T(8,128)(2,1)S(1)} %get-tuple-element.25), channel_id=1, source_target_pairs={{0,4},{4,8},{8,12},{12,14},{14,10},{10,6},{6,2},{2,0},{1,5},{5,9},... | collective-permute-start | bytes 393224 | tf_op jit(solution)/shard_map/ppermute | solution.py:255
  172.5 8.7 %collective-permute-start.30 = (bf16[32,2048]{1,0:T(8,128)(2,1)S(1)}, bf16[32,2048]{1,0:T(8,128)(2,1)S(1)}, u32[]{:S(2)}, u32[]{:S(2)}) collective-permute-start(bf16[32,2048]{1,0:T(8,128)(2,1)S(1)} %get-tuple-element.26), channel_id=1, source_target_pairs={{4,0},{8,4},{12,8},{14,12},{10,14},{6,10},{2,6},{0,2},{5,1},{9,5},... | collective-permute-start | bytes 393224 | tf_op jit(solution)/shard_map/ppermute | solution.py:256
  173.1 20.3 %collective-permute-start.14 = (bf16[32,4096]{1,0:T(8,128)(2,1)S(1)}, bf16[32,4096]{1,0:T(8,128)(2,1)S(1)}, u32[]{:S(2)}, u32[]{:S(2)}) collective-permute-start(bf16[32,4096]{1,0:T(8,128)(2,1)S(1)} %pad_maximum_fusion.2), channel_id=1, source_target_pairs={{4,0},{8,4},{12,8},{14,12},{10,14},{6,10},{2,6},{0,2},{5,1},{9,5},... | collective-permute-start | bytes 786440 | tf_op jit(solution)/shard_map/ppermute | solution.py:265
  177.1 9.2 %collective-permute-start.10 = (bf16[32,4096]{1,0:T(8,128)(2,1)S(1)}, bf16[32,4096]{1,0:T(8,128)(2,1)S(1)}, u32[]{:S(2)}, u32[]{:S(2)}) collective-permute-start(bf16[32,4096]{1,0:T(8,128)(2,1)S(1)} %pad_maximum_fusion.1), channel_id=1, source_target_pairs={{0,4},{4,8},{8,12},{12,14},{14,10},{10,6},{6,2},{2,0},{1,5},{5,9},... | collective-permute-start | bytes 786440 | tf_op jit(solution)/shard_map/ppermute | solution.py:264
  181.3 18.5 %collective-permute-start.31 = (bf16[32,4096]{1,0:T(8,128)(2,1)S(1)}, bf16[32,4096]{1,0:T(8,128)(2,1)S(1)}, u32[]{:S(2)}, u32[]{:S(2)}) collective-permute-start(bf16[32,4096]{1,0:T(8,128)(2,1)S(1)} %pad_maximum_fusion.4), channel_id=1, source_target_pairs={{4,0},{8,4},{12,8},{14,12},{10,14},{6,10},{2,6},{0,2},{5,1},{9,5},... | collective-permute-start | bytes 786440 | tf_op jit(solution)/shard_map/ppermute | solution.py:265
  181.4 10.6 %collective-permute-start.27 = (bf16[32,4096]{1,0:T(8,128)(2,1)S(1)}, bf16[32,4096]{1,0:T(8,128)(2,1)S(1)}, u32[]{:S(2)}, u32[]{:S(2)}) collective-permute-start(bf16[32,4096]{1,0:T(8,128)(2,1)S(1)} %pad_maximum_fusion.3), channel_id=1, source_target_pairs={{0,4},{4,8},{8,12},{12,14},{14,10},{10,6},{6,2},{2,0},{1,5},{5,9},... | collective-permute-start | bytes 786440 | tf_op jit(solution)/shard_map/ppermute | solution.py:264
  186.4 11.2 %collective-permute-start.11 = (bf16[32,4096]{1,0:T(8,128)(2,1)S(1)}, bf16[32,4096]{1,0:T(8,128)(2,1)S(1)}, u32[]{:S(2)}, u32[]{:S(2)}) collective-permute-start(bf16[32,4096]{1,0:T(8,128)(2,1)S(1)} %fusion.8), channel_id=1, source_target_pairs={{0,4},{4,8},{8,12},{12,14},{14,10},{10,6},{6,2},{2,0},{1,5},{5,9},... | collective-permute-start | bytes 786440 | tf_op jit(solution)/shard_map/ppermute | solution.py:264
  192.0 11.2 %collective-permute-start.28 = (bf16[32,4096]{1,0:T(8,128)(2,1)S(1)}, bf16[32,4096]{1,0:T(8,128)(2,1)S(1)}, u32[]{:S(2)}, u32[]{:S(2)}) collective-permute-start(bf16[32,4096]{1,0:T(8,128)(2,1)S(1)} %fusion.2), channel_id=1, source_target_pairs={{0,4},{4,8},{8,12},{12,14},{14,10},{10,6},{6,2},{2,0},{1,5},{5,9},... | collective-permute-start | bytes 786440 | tf_op jit(solution)/shard_map/ppermute | solution.py:264
  197.7 7.7 %collective-permute-start.15 = (bf16[32,4096]{1,0:T(8,128)(2,1)S(1)}, bf16[32,4096]{1,0:T(8,128)(2,1)S(1)}, u32[]{:S(2)}, u32[]{:S(2)}) collective-permute-start(bf16[32,4096]{1,0:T(8,128)(2,1)S(1)} %get-tuple-element.14), channel_id=1, source_target_pairs={{4,0},{8,4},{12,8},{14,12},{10,14},{6,10},{2,6},{0,2},{5,1},{9,5},... | collective-permute-start | bytes 786440 | tf_op jit(solution)/shard_map/ppermute | solution.py:265
  199.7 15.0 %collective-permute-start.12 = (bf16[32,4096]{1,0:T(8,128)(2,1)S(1)}, bf16[32,4096]{1,0:T(8,128)(2,1)S(1)}, u32[]{:S(2)}, u32[]{:S(2)}) collective-permute-start(bf16[32,4096]{1,0:T(8,128)(2,1)S(1)} %get-tuple-element.13), channel_id=1, source_target_pairs={{0,4},{4,8},{8,12},{12,14},{14,10},{10,6},{6,2},{2,0},{1,5},{5,9},... | collective-permute-start | bytes 786440 | tf_op jit(solution)/shard_map/ppermute | solution.py:264
  203.3 9.3 %collective-permute-start.32 = (bf16[32,4096]{1,0:T(8,128)(2,1)S(1)}, bf16[32,4096]{1,0:T(8,128)(2,1)S(1)}, u32[]{:S(2)}, u32[]{:S(2)}) collective-permute-start(bf16[32,4096]{1,0:T(8,128)(2,1)S(1)} %get-tuple-element.18), channel_id=1, source_target_pairs={{4,0},{8,4},{12,8},{14,12},{10,14},{6,10},{2,6},{0,2},{5,1},{9,5},... | collective-permute-start | bytes 786440 | tf_op jit(solution)/shard_map/ppermute | solution.py:265
  205.3 12.9 %collective-permute-start.29 = (bf16[32,4096]{1,0:T(8,128)(2,1)S(1)}, bf16[32,4096]{1,0:T(8,128)(2,1)S(1)}, u32[]{:S(2)}, u32[]{:S(2)}) collective-permute-start(bf16[32,4096]{1,0:T(8,128)(2,1)S(1)} %get-tuple-element.17), channel_id=1, source_target_pairs={{0,4},{4,8},{8,12},{12,14},{14,10},{10,6},{6,2},{2,0},{1,5},{5,9},... | collective-permute-start | bytes 786440 | tf_op jit(solution)/shard_map/ppermute | solution.py:264
  205.4 12.7 %collective-permute-start.16 = (bf16[32,4096]{1,0:T(8,128)(2,1)S(1)}, bf16[32,4096]{1,0:T(8,128)(2,1)S(1)}, u32[]{:S(2)}, u32[]{:S(2)}) collective-permute-start(bf16[32,4096]{1,0:T(8,128)(2,1)S(1)} %fusion.7), channel_id=1, source_target_pairs={{4,0},{8,4},{12,8},{14,12},{10,14},{6,10},{2,6},{0,2},{5,1},{9,5},... | collective-permute-start | bytes 786440 | tf_op jit(solution)/shard_map/ppermute | solution.py:265
  212.7 8.3 %collective-permute-start.33 = (bf16[32,4096]{1,0:T(8,128)(2,1)S(1)}, bf16[32,4096]{1,0:T(8,128)(2,1)S(1)}, u32[]{:S(2)}, u32[]{:S(2)}) collective-permute-start(bf16[32,4096]{1,0:T(8,128)(2,1)S(1)} %fusion.1), channel_id=1, source_target_pairs={{4,0},{8,4},{12,8},{14,12},{10,14},{6,10},{2,6},{0,2},{5,1},{9,5},... | collective-permute-start | bytes 786440 | tf_op jit(solution)/shard_map/ppermute | solution.py:265

commit v2 on v0

v2 whole, which is shorter than its diff:
```python
import functools

import jax
import jax.numpy as jnp
from jax import lax
from jax.experimental import pallas as pl
from jax.experimental.pallas import tpu as pltpu
from jax.sharding import PartitionSpec as P

SIDE = 128
DEPTH = 2
ITEMS = 8
AHEAD = 4
CHUNKS = 2
F32 = jnp.float32
BF16 = jnp.bfloat16


def round_up(n, unit):
    return -(-n // unit) * unit


def kept_items(mask):
    deep, wide = mask.shape
    kept = (mask != 0).astype(jnp.int32).T
    row = jnp.arange(deep)
    before = jnp.sum(jnp.where(row[None, :, None] > row[None, None, :], kept[:, None, :], 0), axis=2)
    filled = round_up(jnp.sum(kept, axis=1), DEPTH)
    column = jnp.arange(wide)
    ends = jnp.sum(jnp.where(column[:, None] >= column[None, :], filled[None, :], 0), axis=1)
    place = jnp.where(kept != 0, (ends - filled)[:, None] + before, -1)
    spots = jnp.arange(round_up(wide * round_up(deep, DEPTH), DEPTH * ITEMS))
    rows = deep + jnp.sum(
        jnp.where(place[None] == spots[:, None, None], row[None, None, :] - deep, 0), axis=(1, 2)
    )
    columns = jnp.sum((ends[None, :] <= spots[::DEPTH][:, None]).astype(jnp.int32), axis=1)
    trips = round_up(ends[-1:], DEPTH * ITEMS) // (DEPTH * ITEMS)
    return rows.astype(jnp.int32), jnp.minimum(columns, wide - 1).astype(jnp.int32), trips.astype(jnp.int32)


def block_of(i):
    return pl.ds(pl.multiple_of(i * SIDE, SIDE), SIDE)


def start_fetches(k, rows, columns, weight, fetched, sems):
    deep = weight.shape[0] // SIDE
    for t in range(ITEMS):
        item = k * ITEMS + t
        column = columns[item]
        for d in range(DEPTH):
            i = rows[item * DEPTH + d]
            i = jnp.where(i == deep, 0, i)
            pltpu.make_async_copy(
                weight.at[block_of(i), block_of(column)],
                fetched.at[block_of(item * DEPTH + d), :],
                sems.at[lax.rem(k, 2 * AHEAD)],
            ).start()


def first_fetches(rows, columns, trips, weight, fetched, sems):
    lax.fori_loop(
        0,
        jnp.minimum(AHEAD, trips[0]),
        lambda k, _: (start_fetches(k, rows, columns, weight, fetched, sems), 0)[1],
        0,
    )


def multiply(rows, columns, trips, weight, held, fetched, sems, total):
    def trip(k, _):
        @pl.when(k + AHEAD < trips[0])
        def _():
            start_fetches(k + AHEAD, rows, columns, weight, fetched, sems)

        span = ITEMS * DEPTH * SIDE
        here = fetched.at[pl.ds(pl.multiple_of(k * span, span), span), :]
        pltpu.make_async_copy(here, here, sems.at[lax.rem(k, 2 * AHEAD)]).wait()
        for t in range(ITEMS):
            item = k * ITEMS + t
            lhs = jnp.concatenate([held[:, block_of(rows[item * DEPTH + d])] for d in range(DEPTH)], axis=1)
            deep = DEPTH * SIDE
            rhs = fetched[pl.ds(pl.multiple_of(item * deep, deep), deep), :]
            total[:, block_of(columns[item])] += jnp.dot(lhs, rhs, preferred_element_type=F32)
        return 0

    lax.fori_loop(0, trips[0], trip, 0)


def scratch(rows, deep, spots):
    return [
        pltpu.VMEM((rows, deep + SIDE), BF16),
        pltpu.VMEM((spots * SIDE, SIDE), BF16),
        pltpu.SemaphoreType.DMA((2 * AHEAD,)),
    ]


SMEM = pl.BlockSpec(memory_space=pltpu.SMEM)
VMEM = pl.BlockSpec(memory_space=pltpu.VMEM)
ANY = pl.BlockSpec(memory_space=pl.ANY)


def tokens_kernel(places, rows, columns, trips, *refs):
    pieces = refs[: len(places)]
    weight, out, held, fetched, sems, piece_sems = refs[len(places) :]
    copies = [
        pltpu.make_async_copy(
            piece, held.at[pl.ds(row, piece.shape[0]), pl.ds(column, piece.shape[1])], piece_sems.at[k]
        )
        for k, (piece, (row, column)) in enumerate(zip(pieces, places))
    ]
    for copy in copies:
        copy.start()
    first_fetches(rows, columns, trips, weight, fetched, sems)
    held[:, weight.shape[0] :] = jnp.zeros((held.shape[0], SIDE), BF16)
    out[...] = jnp.zeros(out.shape, F32)
    for copy in copies:
        copy.wait()
    multiply(rows, columns, trips, weight, held, fetched, sems, out)


def tokens_product(items, pieces, places, weight):
    deep, width = weight.shape
    rows = max(row + piece.shape[0] for piece, (row, _) in zip(pieces, places))
    return pl.pallas_call(
        functools.partial(tokens_kernel, places),
        out_shape=jax.ShapeDtypeStruct((rows, width), F32),
        in_specs=[SMEM] * 3 + [ANY] * (len(pieces) + 1),
        out_specs=VMEM,
        scratch_shapes=scratch(rows, deep, items[0].shape[0]) + [pltpu.SemaphoreType.DMA((len(pieces),))],
        compiler_params=pltpu.CompilerParams(vmem_limit_bytes=40 << 20),
        cost_estimate=pl.CostEstimate(
            flops=rows * deep * width * 2, bytes_accessed=deep * width * 2, transcendentals=0
        ),
    )(*items, *pieces, weight)


SPLIT = 4


def down_kernel(far, rows, columns, trips, *refs):
    sums = refs[:4]
    down, out, on, back, held, fetched, sems, total, *parts, sum_sems = refs[4:]
    count = held.shape[0] // SPLIT

    def copies(r):
        at = pl.ds(r * count, count)
        return [pltpu.make_async_copy(sums[s].at[at], parts[s].at[at], sum_sems.at[r, s]) for s in range(4)]

    for r in range(SPLIT):
        for copy in copies(r):
            copy.start()
    first_fetches(rows, columns, trips, down, fetched, sems)
    deep = down.shape[0]
    held[:, deep:] = jnp.zeros((held.shape[0], SIDE), BF16)
    total[...] = jnp.zeros(total.shape, F32)
    for r in range(SPLIT):
        for copy in copies(r):
            copy.wait()

        def some(s, _, r=r):
            at = pl.ds(pl.multiple_of(r * count + s * 16, 16), 16)
            gate = parts[0][at, :] + parts[1][at, :]
            up = parts[2][at, :] + parts[3][at, :]
            held[at, pl.ds(0, deep)] = (gate / (1.0 + jnp.exp(-gate)) * up).astype(BF16)
            return 0

        lax.fori_loop(0, count // 16, some, 0)
    multiply(rows, columns, trips, down, held, fetched, sems, total)
    near = out.shape[0]
    half = on.shape[1]
    out[...] = total[pl.ds(0, near), :]
    on[...] = total[pl.ds(near, far), pl.ds(0, half)].astype(BF16)
    back[...] = total[pl.ds(near, far), pl.ds(half, half)].astype(BF16)


def down_product(items, sums, down, far):
    deep, width = down.shape
    rows = sums[0].shape[0]
    halves = jax.ShapeDtypeStruct((far, width // 2), BF16)
    return pl.pallas_call(
        functools.partial(down_kernel, far),
        out_shape=(jax.ShapeDtypeStruct((rows - far, width), F32), halves, halves),
        in_specs=[SMEM] * 3 + [ANY] * 5,
        out_specs=(VMEM, VMEM, VMEM),
        scratch_shapes=scratch(rows, deep, items[0].shape[0])
        + [pltpu.VMEM((rows, width), F32)]
        + [pltpu.VMEM((rows, deep), F32)] * 4
        + [pltpu.SemaphoreType.DMA((SPLIT, 4))],
        compiler_params=pltpu.CompilerParams(vmem_limit_bytes=50 << 20),
        cost_estimate=pl.CostEstimate(
            flops=rows * deep * width * 2, bytes_accessed=deep * width * 2, transcendentals=rows * deep
        ),
    )(*items, *sums, down)


def ring_of(n):
    order = list(range(n)) if n > 8 else list(range(0, n, 2)) + list(range(n - 1, 0, -2))
    onward = [(order[k], order[(k + 1) % n]) for k in range(n)]
    return onward, [(b, a) for a, b in onward]


def gather(block, onward, back, n):
    behind, ahead = [block], [block]
    for _ in range(n // 2 - 1):
        behind.append(lax.ppermute(behind[-1], "row", onward))
        ahead.append(lax.ppermute(ahead[-1], "row", back))
    half = block.shape[1] // 2
    left = lax.ppermute(behind[-1][:, :half], "row", onward)
    right = lax.ppermute(ahead[-1][:, half:], "row", back)
    return behind + ahead[1:], (left, right)


def scatter(near, on, ba, rows, onward, back, n):
    half = near.shape[1] // 2
    far = n // 2

    def block(k):
        at = -k if k <= 0 else far - 1 + k
        return near[at * rows : (at + 1) * rows]

    on = lax.ppermute(on, "row", onward)
    ba = lax.ppermute(ba, "row", back)
    for k in range(far - 1, 0, -1):
        if k == far - 1:
            on_sum = jnp.concatenate((block(k)[:, :half] + on.astype(F32), block(k)[:, half:]), axis=1)
            ba_sum = jnp.concatenate((block(-k)[:, :half], block(-k)[:, half:] + ba.astype(F32)), axis=1)
        else:
            on_sum = block(k) + on.astype(F32)
            ba_sum = block(-k) + ba.astype(F32)
        on = lax.ppermute(on_sum.astype(BF16), "row", onward)
        ba = lax.ppermute(ba_sum.astype(BF16), "row", back)
    return (block(0) + on.astype(F32) + ba.astype(F32)).astype(BF16)


def body(n, tokens, gate, up, down, gate_mask, up_mask, down_mask):
    onward, back = ring_of(n)
    swap = [(0, 1), (1, 0)]
    rows = tokens.shape[0] // CHUNKS
    half = tokens.shape[1] // 2
    gate_items, up_items, down_items = kept_items(gate_mask), kept_items(up_mask), kept_items(down_mask)

    outs = []
    for c in range(CHUNKS):
        blocks, (left, right) = gather(tokens[c * rows : (c + 1) * rows], onward, back, n)
        pieces = blocks + [left, right]
        places = [(k * rows, 0) for k in range(n - 1)] + [((n - 1) * rows, 0), ((n - 1) * rows, half)]
        gates = tokens_product(gate_items, pieces, places, gate)
        ups = tokens_product(up_items, pieces, places, up)
        sums = (gates, lax.ppermute(gates, "col", swap), ups, lax.ppermute(ups, "col", swap))
        outs.append(scatter(*down_product(down_items, sums, down, rows), rows, onward, back, n))
    return jnp.concatenate(outs, axis=0)


def solution(mesh):
    return jax.shard_map(
        functools.partial(body, mesh.shape["row"]),
        mesh=mesh,
        in_specs=(
            P(("groups", "row"), "col"),
            P("col", "row"),
            P("col", "row"),
            P("row", "col"),
            P("col", "row"),
            P("col", "row"),
            P("row", "col"),
        ),
        out_specs=P(("groups", "row"), "col"),
        check_vma=False,
    )
```

time: 342 us -> 155 us (0.45)
  waiting for transfers between devices: 188 us -> 45.4 us
  local copies, waits for them, and re-layouts: 61.3 us -> 5.56 us
  Pallas kernels: 0 us -> 51.5 us
  matrix products: 40.9 us -> 0 us
  starting transfers between devices: 0.26 us -> 37.9 us
  other arithmetic: 37.2 us -> 10.6 us
  between operations: 13.1 us -> 4.53 us
    reduce_scatter x1 -> x0, waiting for transfers between devices: 150 us -> none  [body(): lax.psum_scatter(jnp.dot(hidden, down_kept, preferred_element_type=jnp.fl...]
    pallas_call x0 -> x6, Pallas kernels: none -> 51.5 us  [the longest x4 27 us: tokens_product(): pl.pallas_call(functools.partial(tokens_kernel, places), out_shape=jax.Sh...]
    ppermute x0 -> x36, waiting for transfers between devices: none -> 45.4 us  [the longest x6 15.3 us: scatter(): on = lax.ppermute(on_sum.astype(BF16), 'row', onward)]
    dot_general x2 -> x0, matrix products: 40.9 us -> none  [the longest x1 22.5 us: body(): jnp.dot(lax.all_gather(tokens, 'row', axis=0, tiled=True), both_kept, pre...]
    ppermute x0 -> x36, starting transfers between devices: none -> 37.9 us  [the longest x6 13.6 us: gather(): behind.append(lax.ppermute(behind[-1], 'row', onward))]
    unnamed x4 -> x12, local copies, waits for them, and re-layouts: 39.9 us -> 2.45 us
    psum x1 -> x0, waiting for transfers between devices: 36.7 us -> none  [body(): summed = lax.psum(partial_sums, 'col')]
    mul x1 -> x3, other arithmetic: 33.7 us -> 0.04 us  [round_up(): return -(-n // unit) * unit]
  transfers between devices with their start and end apart: 3 -> 36, of which waited for: 2 -> 13; matrix products, arithmetic and copies ran while one was open for 26% -> 8% of each run, Pallas kernels for 0% -> 33%
where the time goes in v2:
time: 155 us
  Pallas kernels  51.5 us (33%)
  waiting for transfers between devices  45.4 us (29%)
  starting transfers between devices  37.9 us (24%)
  other arithmetic  10.6 us (7%)
  local copies, waits for them, and re-layouts  5.56 us (4%)
  between operations  4.53 us (3%)
    pallas_call x4, Pallas kernels, tokens_product(): pl.pallas_call(functools.partial(tokens_kernel, places), out_shape=jax.Sh...  27 us
    pallas_call x2, Pallas kernels, down_product(): pl.pallas_call(functools.partial(down_kernel, far), out_shape=(jax.ShapeD...  24.5 us
    ppermute x6, waiting for transfers between devices, scatter(): on = lax.ppermute(on_sum.astype(BF16), 'row', onward)  15.3 us
    ppermute x6, waiting for transfers between devices, scatter(): ba = lax.ppermute(ba_sum.astype(BF16), 'row', back)  15.2 us
    ppermute x6, waiting for transfers between devices, gather(): behind.append(lax.ppermute(behind[-1], 'row', onward))  14.7 us
    ppermute x6, starting transfers between devices, gather(): behind.append(lax.ppermute(behind[-1], 'row', onward))  13.6 us
    ppermute x6, starting transfers between devices, scatter(): on = lax.ppermute(on_sum.astype(BF16), 'row', onward)  11.6 us
    another operation x4, other arithmetic  4.81 us
  transfers between devices with their start and end apart: 36, of which 13 were waited for; matrix products, arithmetic and copies ran while one was open for 8% of the time, Pallas kernels for 33%

profile of v2, /device:TPU:0, one launch (start us, length us, event | category | flops | bytes accessed | tf_op | source)
XLA Modules:
  0.0 155.5 jit_solution(14080403690967546798)
XLA Ops:
  0.0 1.1 fusion.2
  1.1 3.1 %collective-permute-start = (bf16[32,4096]{1,0:T(8,128)(2,1)S(1)}, bf16[32,4096]{1,0:T(8,128)(2,1)S(1)}, u32[]{:S(2)}, u32[]{:S(2)}) collective-permute-start(bf16[32,4096]{1,0:T(8,128)(2,1)S(1)} %get-tuple-element.41.refs_0_), channel_id=1, source_target_pairs={{0,4},{4,8},{8,12},{12,14},{14,10},{10,6},{6,2},{2,0},{1,5},{5,9},... | collective-permute-start | bytes 786440 | tf_op jit(solution)/shard_map/ppermute | solution.py:205
  4.2 2.0 %collective-permute-start.18 = (bf16[32,4096]{1,0:T(8,128)(2,1)S(1)}, bf16[32,4096]{1,0:T(8,128)(2,1)S(1)}, u32[]{:S(2)}, u32[]{:S(2)}) collective-permute-start(bf16[32,4096]{1,0:T(8,128)(2,1)S(1)} %get-tuple-element.42.refs_0_), channel_id=1, source_target_pairs={{0,4},{4,8},{8,12},{12,14},{14,10},{10,6},{6,2},{2,0},{1,5},{5,9},... | collective-permute-start | bytes 786440 | tf_op jit(solution)/shard_map/ppermute | solution.py:205
  6.2 0.8 convert_reduce_fusion.3
  7.0 0.1 select_reduce_fusion.7
  7.1 0.8 convert_reduce_fusion.4
  8.0 0.1 select_reduce_fusion.8
  8.1 0.5 select_reduce_fusion.3
  8.8 0.3 select_reduce_fusion
  9.1 0.2 slice.110
  9.4 0.7 convert_reduce_fusion.5
  10.1 1.1 collective-permute-done.refs_1_
  11.2 2.1 %collective-permute-start.1 = (bf16[32,4096]{1,0:T(8,128)(2,1)S(1)}, bf16[32,4096]{1,0:T(8,128)(2,1)S(1)}, u32[]{:S(2)}, u32[]{:S(2)}) collective-permute-start(bf16[32,4096]{1,0:T(8,128)(2,1)S(1)} %collective-permute-done.refs_1_), channel_id=1, source_target_pairs={{0,4},{4,8},{8,12},{12,14},{14,10},{10,6},{6,2},{2,0},{1,5},{5,9},... | collective-permute-start | bytes 786440 | tf_op jit(solution)/shard_map/ppermute | solution.py:205
  13.4 3.5 %collective-permute-done.18.refs_1_ = bf16[32,4096]{1,0:T(8,128)(2,1)S(1)} collective-permute-done((bf16[32,4096]{1,0:T(8,128)(2,1)S(1)}, bf16[32,4096]{1,0:T(8,128)(2,1)S(1)}, u32[]{:S(2)}, u32[]{:S(2)}) %collective-permute-start.18) | collective-permute-done | bytes 262176 | tf_op jit(solution)/shard_map/ppermute | solution.py:205
  16.8 2.1 %collective-permute-start.19 = (bf16[32,4096]{1,0:T(8,128)(2,1)S(1)}, bf16[32,4096]{1,0:T(8,128)(2,1)S(1)}, u32[]{:S(2)}, u32[]{:S(2)}) collective-permute-start(bf16[32,4096]{1,0:T(8,128)(2,1)S(1)} %collective-permute-done.18.refs_1_), channel_id=1, source_target_pairs={{0,4},{4,8},{8,12},{12,14},{14,10},{10,6},{6,2},{2,0},{1,5},{5,9},... | collective-permute-start | bytes 786440 | tf_op jit(solution)/shard_map/ppermute | solution.py:205
  19.0 3.5 %collective-permute-done.1.refs_2_ = bf16[32,4096]{1,0:T(8,128)(2,1)S(1)} collective-permute-done((bf16[32,4096]{1,0:T(8,128)(2,1)S(1)}, bf16[32,4096]{1,0:T(8,128)(2,1)S(1)}, u32[]{:S(2)}, u32[]{:S(2)}) %collective-permute-start.1) | collective-permute-done | bytes 262176 | tf_op jit(solution)/shard_map/ppermute | solution.py:205
  22.5 2.1 %collective-permute-start.2 = (bf16[32,4096]{1,0:T(8,128)(2,1)S(1)}, bf16[32,4096]{1,0:T(8,128)(2,1)S(1)}, u32[]{:S(2)}, u32[]{:S(2)}) collective-permute-start(bf16[32,4096]{1,0:T(8,128)(2,1)S(1)} %collective-permute-done.1.refs_2_), channel_id=1, source_target_pairs={{0,4},{4,8},{8,12},{12,14},{14,10},{10,6},{6,2},{2,0},{1,5},{5,9},... | collective-permute-start | bytes 786440 | tf_op jit(solution)/shard_map/ppermute | solution.py:205
  24.6 0.1 select_reduce_fusion.6
  24.7 3.3 %collective-permute-done.19.refs_2_ = bf16[32,4096]{1,0:T(8,128)(2,1)S(1)} collective-permute-done((bf16[32,4096]{1,0:T(8,128)(2,1)S(1)}, bf16[32,4096]{1,0:T(8,128)(2,1)S(1)}, u32[]{:S(2)}, u32[]{:S(2)}) %collective-permute-start.19) | collective-permute-done | bytes 262176 | tf_op jit(solution)/shard_map/ppermute | solution.py:205
  28.1 2.1 %collective-permute-start.20 = (bf16[32,4096]{1,0:T(8,128)(2,1)S(1)}, bf16[32,4096]{1,0:T(8,128)(2,1)S(1)}, u32[]{:S(2)}, u32[]{:S(2)}) collective-permute-start(bf16[32,4096]{1,0:T(8,128)(2,1)S(1)} %collective-permute-done.19.refs_2_), channel_id=1, source_target_pairs={{0,4},{4,8},{8,12},{12,14},{14,10},{10,6},{6,2},{2,0},{1,5},{5,9},... | collective-permute-start | bytes 786440 | tf_op jit(solution)/shard_map/ppermute | solution.py:205
  30.3 3.4 %collective-permute-done.2.refs_3_ = bf16[32,4096]{1,0:T(8,128)(2,1)S(1)} collective-permute-done((bf16[32,4096]{1,0:T(8,128)(2,1)S(1)}, bf16[32,4096]{1,0:T(8,128)(2,1)S(1)}, u32[]{:S(2)}, u32[]{:S(2)}) %collective-permute-start.2) | collective-permute-done | bytes 262176 | tf_op jit(solution)/shard_map/ppermute | solution.py:205
  33.7 2.2 %collective-permute-start.6 = (bf16[32,2048]{1,0:T(8,128)(2,1)S(1)}, bf16[32,2048]{1,0:T(8,128)(2,1)S(1)}, u32[]{:S(2)}, u32[]{:S(2)}) collective-permute-start(bf16[32,2048]{1,0:T(8,128)(2,1)S(1)} %slice.138), channel_id=1, source_target_pairs={{0,4},{4,8},{8,12},{12,14},{14,10},{10,6},{6,2},{2,0},{1,5},{5,9},... | collective-permute-start | bytes 393224 | tf_op jit(solution)/shard_map/ppermute | solution.py:208
  36.0 0.6 slice.116
  37.9 0.6 slice.112
  39.8 0.6 slice.111
  41.7 0.1 select_reduce_fusion.5
  41.9 2.1 %collective-permute-start.24 = (bf16[32,2048]{1,0:T(8,128)(2,1)S(1)}, bf16[32,2048]{1,0:T(8,128)(2,1)S(1)}, u32[]{:S(2)}, u32[]{:S(2)}) collective-permute-start(bf16[32,2048]{1,0:T(8,128)(2,1)S(1)} %slice.142), channel_id=1, source_target_pairs={{0,4},{4,8},{8,12},{12,14},{14,10},{10,6},{6,2},{2,0},{1,5},{5,9},... | collective-permute-start | bytes 393224 | tf_op jit(solution)/shard_map/ppermute | solution.py:208
  44.1 6.5 %shard_map.74.refs_2_ = f32[256,1792]{1,0:T(8,128)S(1)} custom-call(s32[448]{0:T(512)S(1)} %broadcast_add_fusion.rows, s32[224]{0:T(256)S(1)} %broadcast_minimum_fusion.columns, s32[1]{0:T(128)S(6)} %select_n.121.trips, bf16[32,4096]{1,0:T(8,128)(2,1)S(1)} %get-tuple-element.41.refs_0_, bf16[32,4096]{1,0:T(8,128)(2,1)S(1)} %collective-permute-done.refs_1_, ...), custom_call_target="tpu_custom_call" | custom-call | flops 3758096384 | bytes 14680064 | tf_op jit(solution)/shard_map/pallas_call | solution.py:124
  50.6 7.0 %shard_map.73.refs_0_ = f32[256,1792]{1,0:T(8,128)S(1)} custom-call(s32[448]{0:T(512)S(1)} %broadcast_add_fusion.1.rows, s32[224]{0:T(256)S(1)} %broadcast_minimum_fusion.1.columns, s32[1]{0:T(128)S(6)} %select_n.114.trips, bf16[32,4096]{1,0:T(8,128)(2,1)S(1)} %get-tuple-element.41.refs_0_, bf16[32,4096]{1,0:T(8,128)(2,1)S(1)} %collective-permute-done.refs_1_, ...), custom_call_target="tpu_custom_call" | custom-call | flops 3758096384 | bytes 14680064 | tf_op jit(solution)/shard_map/pallas_call | solution.py:124
  57.7 1.4 collective-permute-start.8
  59.1 6.5 %shard_map.77.refs_2_ = f32[256,1792]{1,0:T(8,128)S(1)} custom-call(s32[448]{0:T(512)S(1)} %broadcast_add_fusion.rows, s32[224]{0:T(256)S(1)} %broadcast_minimum_fusion.columns, s32[1]{0:T(128)S(6)} %select_n.121.trips, bf16[32,4096]{1,0:T(8,128)(2,1)S(1)} %get-tuple-element.42.refs_0_, bf16[32,4096]{1,0:T(8,128)(2,1)S(1)} %collective-permute-done.18.refs_1_, ...), custom_call_target="tpu_custom_call" | custom-call | flops 3758096384 | bytes 14680064 | tf_op jit(solution)/shard_map/pallas_call | solution.py:124
  65.6 0.6 collective-permute-start.27
  66.3 7.0 %shard_map.76.refs_0_ = f32[256,1792]{1,0:T(8,128)S(1)} custom-call(s32[448]{0:T(512)S(1)} %broadcast_add_fusion.1.rows, s32[224]{0:T(256)S(1)} %broadcast_minimum_fusion.1.columns, s32[1]{0:T(128)S(6)} %select_n.114.trips, bf16[32,4096]{1,0:T(8,128)(2,1)S(1)} %get-tuple-element.42.refs_0_, bf16[32,4096]{1,0:T(8,128)(2,1)S(1)} %collective-permute-done.18.refs_1_, ...), custom_call_target="tpu_custom_call" | custom-call | flops 3758096384 | bytes 14680064 | tf_op jit(solution)/shard_map/pallas_call | solution.py:124
  73.3 1.0 collective-permute-start.26
  74.3 0.2 select_reduce_fusion.2
  74.5 1.2 copy-done.4
  75.7 12.2 %shard_map.75 = (f32[224,4096]{1,0:T(8,128)}, bf16[32,2048]{1,0:T(8,128)(2,1)S(1)}, bf16[32,2048]{1,0:T(8,128)(2,1)S(1)}) custom-call(s32[448]{0:T(512)S(1)} %broadcast_add_fusion.2.rows, s32[224]{0:T(256)S(1)} %broadcast_minimum_fusion.2.columns, s32[1]{0:T(128)S(6)} %select_n.107.trips, f32[256,1792]{1,0:T(8,128)S(1)} %shard_map.73.refs_0_, ...), custom_call_target="tpu_custom_call" | custom-call | flops 3758096384 | bytes 14680064 | tf_op jit(solution)/shard_map/pallas_call | solution.py:180
  88.0 0.9 collective-permute-start.10
  88.9 1.2 collective-permute-start.14
  90.1 2.3 %convert.25 = bf16[224,4096]{1,0:T(8,128)(2,1)S(1)} convert(f32[224,4096]{1,0:T(8,128)} %get-tuple-element.11) | non-fusion elementwise | flops 917504 | bytes 5505024 | tf_op jit(solution)/shard_map/convert.11
  92.4 1.2 copy-done.5
  93.6 12.3 %shard_map.78 = (f32[224,4096]{1,0:T(8,128)}, bf16[32,2048]{1,0:T(8,128)(2,1)S(1)}, bf16[32,2048]{1,0:T(8,128)(2,1)S(1)}) custom-call(s32[448]{0:T(512)S(1)} %broadcast_add_fusion.2.rows, s32[224]{0:T(256)S(1)} %broadcast_minimum_fusion.2.columns, s32[1]{0:T(128)S(6)} %select_n.107.trips, f32[256,1792]{1,0:T(8,128)S(1)} %shard_map.76.refs_0_, ...), custom_call_target="tpu_custom_call" | custom-call | flops 3758096384 | bytes 14680064 | tf_op jit(solution)/shard_map/pallas_call | solution.py:180
  105.9 1.5 collective-permute-start.28
  107.4 0.6 collective-permute-start.32
  108.0 2.4 %convert.28 = bf16[224,4096]{1,0:T(8,128)(2,1)S(1)} convert(f32[224,4096]{1,0:T(8,128)} %get-tuple-element.14) | non-fusion elementwise | flops 917504 | bytes 5505024 | tf_op jit(solution)/shard_map/convert.5
  110.6 2.1 %collective-permute-start.11 = (bf16[32,4096]{1,0:T(8,128)(2,1)S(1)}, bf16[32,4096]{1,0:T(8,128)(2,1)S(1)}, u32[]{:S(2)}, u32[]{:S(2)}) collective-permute-start(bf16[32,4096]{1,0:T(8,128)(2,1)S(1)} %pad_maximum_fusion.1), channel_id=1, source_target_pairs={{0,4},{4,8},{8,12},{12,14},{14,10},{10,6},{6,2},{2,0},{1,5},{5,9},... | collective-permute-start | bytes 786440 | tf_op jit(solution)/shard_map/ppermute | solution.py:230
  112.8 0.8 collective-permute-start.33
  113.7 1.3 collective-permute-start.29
  114.9 5.0 %collective-permute-done.11 = bf16[32,4096]{1,0:T(8,128)(2,1)S(1)} collective-permute-done((bf16[32,4096]{1,0:T(8,128)(2,1)S(1)}, bf16[32,4096]{1,0:T(8,128)(2,1)S(1)}, u32[]{:S(2)}, u32[]{:S(2)}) %collective-permute-start.11) | collective-permute-done | bytes 262176 | tf_op jit(solution)/shard_map/ppermute | solution.py:230
  120.0 2.1 %collective-permute-start.12 = (bf16[32,4096]{1,0:T(8,128)(2,1)S(1)}, bf16[32,4096]{1,0:T(8,128)(2,1)S(1)}, u32[]{:S(2)}, u32[]{:S(2)}) collective-permute-start(bf16[32,4096]{1,0:T(8,128)(2,1)S(1)} %add_convert_fusion.9), channel_id=1, source_target_pairs={{0,4},{4,8},{8,12},{12,14},{14,10},{10,6},{6,2},{2,0},{1,5},{5,9},... | collective-permute-start | bytes 786440 | tf_op jit(solution)/shard_map/ppermute | solution.py:230
  122.1 3.5 %collective-permute-done.29 = bf16[32,4096]{1,0:T(8,128)(2,1)S(1)} collective-permute-done((bf16[32,4096]{1,0:T(8,128)(2,1)S(1)}, bf16[32,4096]{1,0:T(8,128)(2,1)S(1)}, u32[]{:S(2)}, u32[]{:S(2)}) %collective-permute-start.29) | collective-permute-done | bytes 262176 | tf_op jit(solution)/shard_map/ppermute | solution.py:230
  125.6 2.1 %collective-permute-start.30 = (bf16[32,4096]{1,0:T(8,128)(2,1)S(1)}, bf16[32,4096]{1,0:T(8,128)(2,1)S(1)}, u32[]{:S(2)}, u32[]{:S(2)}) collective-permute-start(bf16[32,4096]{1,0:T(8,128)(2,1)S(1)} %add_convert_fusion.4), channel_id=1, source_target_pairs={{0,4},{4,8},{8,12},{12,14},{14,10},{10,6},{6,2},{2,0},{1,5},{5,9},... | collective-permute-start | bytes 786440 | tf_op jit(solution)/shard_map/ppermute | solution.py:230
  127.7 3.5 %collective-permute-done.12 = bf16[32,4096]{1,0:T(8,128)(2,1)S(1)} collective-permute-done((bf16[32,4096]{1,0:T(8,128)(2,1)S(1)}, bf16[32,4096]{1,0:T(8,128)(2,1)S(1)}, u32[]{:S(2)}, u32[]{:S(2)}) %collective-permute-start.12) | collective-permute-done | bytes 262176 | tf_op jit(solution)/shard_map/ppermute | solution.py:230
  131.2 0.1 add_convert_fusion.8
  131.4 2.1 %collective-permute-start.13 = (bf16[32,4096]{1,0:T(8,128)(2,1)S(1)}, bf16[32,4096]{1,0:T(8,128)(2,1)S(1)}, u32[]{:S(2)}, u32[]{:S(2)}) collective-permute-start(bf16[32,4096]{1,0:T(8,128)(2,1)S(1)} %get-tuple-element.29), channel_id=1, source_target_pairs={{0,4},{4,8},{8,12},{12,14},{14,10},{10,6},{6,2},{2,0},{1,5},{5,9},... | collective-permute-start | bytes 786440 | tf_op jit(solution)/shard_map/ppermute | solution.py:230
  133.4 3.4 %collective-permute-done.30 = bf16[32,4096]{1,0:T(8,128)(2,1)S(1)} collective-permute-done((bf16[32,4096]{1,0:T(8,128)(2,1)S(1)}, bf16[32,4096]{1,0:T(8,128)(2,1)S(1)}, u32[]{:S(2)}, u32[]{:S(2)}) %collective-permute-start.30) | collective-permute-done | bytes 262176 | tf_op jit(solution)/shard_map/ppermute | solution.py:230
  136.8 0.1 add_convert_fusion.3
  137.0 2.1 %collective-permute-start.31 = (bf16[32,4096]{1,0:T(8,128)(2,1)S(1)}, bf16[32,4096]{1,0:T(8,128)(2,1)S(1)}, u32[]{:S(2)}, u32[]{:S(2)}) collective-permute-start(bf16[32,4096]{1,0:T(8,128)(2,1)S(1)} %get-tuple-element.33), channel_id=1, source_target_pairs={{0,4},{4,8},{8,12},{12,14},{14,10},{10,6},{6,2},{2,0},{1,5},{5,9},... | collective-permute-start | bytes 786440 | tf_op jit(solution)/shard_map/ppermute | solution.py:230
  139.0 1.1 collective-permute-done.16
  140.2 6.0 %collective-permute-done.34 = bf16[32,4096]{1,0:T(8,128)(2,1)S(1)} collective-permute-done((bf16[32,4096]{1,0:T(8,128)(2,1)S(1)}, bf16[32,4096]{1,0:T(8,128)(2,1)S(1)}, u32[]{:S(2)}, u32[]{:S(2)}) %collective-permute-start.34) | collective-permute-done | bytes 262176 | tf_op jit(solution)/shard_map/ppermute | solution.py:231
  146.3 5.4 %collective-permute-done.17 = bf16[32,4096]{1,0:T(8,128)(2,1)S(1)} collective-permute-done((bf16[32,4096]{1,0:T(8,128)(2,1)S(1)}, bf16[32,4096]{1,0:T(8,128)(2,1)S(1)}, u32[]{:S(2)}, u32[]{:S(2)}) %collective-permute-start.17) | collective-permute-done | bytes 262176 | tf_op jit(solution)/shard_map/ppermute | solution.py:231
  151.8 0.1 add_convert_fusion.5
  151.9 2.7 %collective-permute-done.35 = bf16[32,4096]{1,0:T(8,128)(2,1)S(1)} collective-permute-done((bf16[32,4096]{1,0:T(8,128)(2,1)S(1)}, bf16[32,4096]{1,0:T(8,128)(2,1)S(1)}, u32[]{:S(2)}, u32[]{:S(2)}) %collective-permute-start.35) | collective-permute-done | bytes 262176 | tf_op jit(solution)/shard_map/ppermute | solution.py:231
  154.7 0.8 pad_maximum_fusion
  (88 shorter events, 1.8 us)
Async XLA Ops:
  1.1 10.2 %collective-permute-start = (bf16[32,4096]{1,0:T(8,128)(2,1)S(1)}, bf16[32,4096]{1,0:T(8,128)(2,1)S(1)}, u32[]{:S(2)}, u32[]{:S(2)}) collective-permute-start(bf16[32,4096]{1,0:T(8,128)(2,1)S(1)} %get-tuple-element.41.refs_0_), channel_id=1, source_target_pairs={{0,4},{4,8},{8,12},{12,14},{14,10},{10,6},{6,2},{2,0},{1,5},{5,9},... | collective-permute-start | bytes 786440 | tf_op jit(solution)/shard_map/ppermute | solution.py:205
  4.1 9.2 %collective-permute-start.3 = (bf16[32,4096]{1,0:T(8,128)(2,1)S(1)}, bf16[32,4096]{1,0:T(8,128)(2,1)S(1)}, u32[]{:S(2)}, u32[]{:S(2)}) collective-permute-start(bf16[32,4096]{1,0:T(8,128)(2,1)S(1)} %get-tuple-element.41.refs_0_), channel_id=1, source_target_pairs={{4,0},{8,4},{12,8},{14,12},{10,14},{6,10},{2,6},{0,2},{5,1},{9,5},... | collective-permute-start | bytes 786440 | tf_op jit(solution)/shard_map/ppermute | solution.py:206
  4.2 12.7 %collective-permute-start.18 = (bf16[32,4096]{1,0:T(8,128)(2,1)S(1)}, bf16[32,4096]{1,0:T(8,128)(2,1)S(1)}, u32[]{:S(2)}, u32[]{:S(2)}) collective-permute-start(bf16[32,4096]{1,0:T(8,128)(2,1)S(1)} %get-tuple-element.42.refs_0_), channel_id=1, source_target_pairs={{0,4},{4,8},{8,12},{12,14},{14,10},{10,6},{6,2},{2,0},{1,5},{5,9},... | collective-permute-start | bytes 786440 | tf_op jit(solution)/shard_map/ppermute | solution.py:205
  6.2 12.8 %collective-permute-start.21 = (bf16[32,4096]{1,0:T(8,128)(2,1)S(1)}, bf16[32,4096]{1,0:T(8,128)(2,1)S(1)}, u32[]{:S(2)}, u32[]{:S(2)}) collective-permute-start(bf16[32,4096]{1,0:T(8,128)(2,1)S(1)} %get-tuple-element.42.refs_0_), channel_id=1, source_target_pairs={{4,0},{8,4},{12,8},{14,12},{10,14},{6,10},{2,6},{0,2},{5,1},{9,5},... | collective-permute-start | bytes 786440 | tf_op jit(solution)/shard_map/ppermute | solution.py:206
  11.2 11.2 %collective-permute-start.1 = (bf16[32,4096]{1,0:T(8,128)(2,1)S(1)}, bf16[32,4096]{1,0:T(8,128)(2,1)S(1)}, u32[]{:S(2)}, u32[]{:S(2)}) collective-permute-start(bf16[32,4096]{1,0:T(8,128)(2,1)S(1)} %collective-permute-done.refs_1_), channel_id=1, source_target_pairs={{0,4},{4,8},{8,12},{12,14},{14,10},{10,6},{6,2},{2,0},{1,5},{5,9},... | collective-permute-start | bytes 786440 | tf_op jit(solution)/shard_map/ppermute | solution.py:205
  13.4 11.2 %collective-permute-start.4 = (bf16[32,4096]{1,0:T(8,128)(2,1)S(1)}, bf16[32,4096]{1,0:T(8,128)(2,1)S(1)}, u32[]{:S(2)}, u32[]{:S(2)}) collective-permute-start(bf16[32,4096]{1,0:T(8,128)(2,1)S(1)} %collective-permute-done.3.refs_4_), channel_id=1, source_target_pairs={{4,0},{8,4},{12,8},{14,12},{10,14},{6,10},{2,6},{0,2},{5,1},{9,5},... | collective-permute-start | bytes 786440 | tf_op jit(solution)/shard_map/ppermute | solution.py:206
  16.8 11.2 %collective-permute-start.19 = (bf16[32,4096]{1,0:T(8,128)(2,1)S(1)}, bf16[32,4096]{1,0:T(8,128)(2,1)S(1)}, u32[]{:S(2)}, u32[]{:S(2)}) collective-permute-start(bf16[32,4096]{1,0:T(8,128)(2,1)S(1)} %collective-permute-done.18.refs_1_), channel_id=1, source_target_pairs={{0,4},{4,8},{8,12},{12,14},{14,10},{10,6},{6,2},{2,0},{1,5},{5,9},... | collective-permute-start | bytes 786440 | tf_op jit(solution)/shard_map/ppermute | solution.py:205
  19.0 11.2 %collective-permute-start.22 = (bf16[32,4096]{1,0:T(8,128)(2,1)S(1)}, bf16[32,4096]{1,0:T(8,128)(2,1)S(1)}, u32[]{:S(2)}, u32[]{:S(2)}) collective-permute-start(bf16[32,4096]{1,0:T(8,128)(2,1)S(1)} %collective-permute-done.21.refs_4_), channel_id=1, source_target_pairs={{4,0},{8,4},{12,8},{14,12},{10,14},{6,10},{2,6},{0,2},{5,1},{9,5},... | collective-permute-start | bytes 786440 | tf_op jit(solution)/shard_map/ppermute | solution.py:206
  22.5 11.2 %collective-permute-start.2 = (bf16[32,4096]{1,0:T(8,128)(2,1)S(1)}, bf16[32,4096]{1,0:T(8,128)(2,1)S(1)}, u32[]{:S(2)}, u32[]{:S(2)}) collective-permute-start(bf16[32,4096]{1,0:T(8,128)(2,1)S(1)} %collective-permute-done.1.refs_2_), channel_id=1, source_target_pairs={{0,4},{4,8},{8,12},{12,14},{14,10},{10,6},{6,2},{2,0},{1,5},{5,9},... | collective-permute-start | bytes 786440 | tf_op jit(solution)/shard_map/ppermute | solution.py:205
  24.6 11.3 %collective-permute-start.5 = (bf16[32,4096]{1,0:T(8,128)(2,1)S(1)}, bf16[32,4096]{1,0:T(8,128)(2,1)S(1)}, u32[]{:S(2)}, u32[]{:S(2)}) collective-permute-start(bf16[32,4096]{1,0:T(8,128)(2,1)S(1)} %collective-permute-done.4.refs_5_), channel_id=1, source_target_pairs={{4,0},{8,4},{12,8},{14,12},{10,14},{6,10},{2,6},{0,2},{5,1},{9,5},... | collective-permute-start | bytes 786440 | tf_op jit(solution)/shard_map/ppermute | solution.py:206
  28.1 13.8 %collective-permute-start.20 = (bf16[32,4096]{1,0:T(8,128)(2,1)S(1)}, bf16[32,4096]{1,0:T(8,128)(2,1)S(1)}, u32[]{:S(2)}, u32[]{:S(2)}) collective-permute-start(bf16[32,4096]{1,0:T(8,128)(2,1)S(1)} %collective-permute-done.19.refs_2_), channel_id=1, source_target_pairs={{0,4},{4,8},{8,12},{12,14},{14,10},{10,6},{6,2},{2,0},{1,5},{5,9},... | collective-permute-start | bytes 786440 | tf_op jit(solution)/shard_map/ppermute | solution.py:205
  30.2 13.7 %collective-permute-start.23 = (bf16[32,4096]{1,0:T(8,128)(2,1)S(1)}, bf16[32,4096]{1,0:T(8,128)(2,1)S(1)}, u32[]{:S(2)}, u32[]{:S(2)}) collective-permute-start(bf16[32,4096]{1,0:T(8,128)(2,1)S(1)} %collective-permute-done.22.refs_5_), channel_id=1, source_target_pairs={{4,0},{8,4},{12,8},{14,12},{10,14},{6,10},{2,6},{0,2},{5,1},{9,5},... | collective-permute-start | bytes 786440 | tf_op jit(solution)/shard_map/ppermute | solution.py:206
  33.7 10.3 %collective-permute-start.6 = (bf16[32,2048]{1,0:T(8,128)(2,1)S(1)}, bf16[32,2048]{1,0:T(8,128)(2,1)S(1)}, u32[]{:S(2)}, u32[]{:S(2)}) collective-permute-start(bf16[32,2048]{1,0:T(8,128)(2,1)S(1)} %slice.138), channel_id=1, source_target_pairs={{0,4},{4,8},{8,12},{12,14},{14,10},{10,6},{6,2},{2,0},{1,5},{5,9},... | collective-permute-start | bytes 393224 | tf_op jit(solution)/shard_map/ppermute | solution.py:208
  35.9 8.2 %collective-permute-start.7 = (bf16[32,2048]{1,0:T(8,128)(2,1)S(1)}, bf16[32,2048]{1,0:T(8,128)(2,1)S(1)}, u32[]{:S(2)}, u32[]{:S(2)}) collective-permute-start(bf16[32,2048]{1,0:T(8,128)(2,1)S(1)} %slice.139), channel_id=1, source_target_pairs={{4,0},{8,4},{12,8},{14,12},{10,14},{6,10},{2,6},{0,2},{5,1},{9,5},... | collective-permute-start | bytes 393224 | tf_op jit(solution)/shard_map/ppermute | solution.py:209
  41.9 17.2 %collective-permute-start.24 = (bf16[32,2048]{1,0:T(8,128)(2,1)S(1)}, bf16[32,2048]{1,0:T(8,128)(2,1)S(1)}, u32[]{:S(2)}, u32[]{:S(2)}) collective-permute-start(bf16[32,2048]{1,0:T(8,128)(2,1)S(1)} %slice.142), channel_id=1, source_target_pairs={{0,4},{4,8},{8,12},{12,14},{14,10},{10,6},{6,2},{2,0},{1,5},{5,9},... | collective-permute-start | bytes 393224 | tf_op jit(solution)/shard_map/ppermute | solution.py:208
  44.0 15.2 %collective-permute-start.25 = (bf16[32,2048]{1,0:T(8,128)(2,1)S(1)}, bf16[32,2048]{1,0:T(8,128)(2,1)S(1)}, u32[]{:S(2)}, u32[]{:S(2)}) collective-permute-start(bf16[32,2048]{1,0:T(8,128)(2,1)S(1)} %slice.143), channel_id=1, source_target_pairs={{4,0},{8,4},{12,8},{14,12},{10,14},{6,10},{2,6},{0,2},{5,1},{9,5},... | collective-permute-start | bytes 393224 | tf_op jit(solution)/shard_map/ppermute | solution.py:209
  50.5 7.1 %copy-start.1 = (f32[256,1792]{1,0:T(8,128)}, f32[256,1792]{1,0:T(8,128)S(1)}, u32[]{:S(2)}) copy-start(f32[256,1792]{1,0:T(8,128)S(1)} %shard_map.74.refs_2_) | copy-start | bytes 5505028
  50.6 23.9 %collective-permute-start.9 = (f32[256,1792]{1,0:T(8,128)S(1)}, f32[256,1792]{1,0:T(8,128)S(1)}, u32[]{:S(2)}, u32[]{:S(2)}) collective-permute-start(f32[256,1792]{1,0:T(8,128)S(1)} %shard_map.74.refs_2_), channel_id=1, source_target_pairs={{0,1},{1,0},{2,3},{3,2},{4,5},{5,4},{6,7},{7,6},{8,9},{9,8},{10,11... | collective-permute-start | bytes 5505032 | tf_op jit(solution)/shard_map/ppermute | solution.py:249
  57.7 16.8 %collective-permute-start.8 = (f32[256,1792]{1,0:T(8,128)S(1)}, f32[256,1792]{1,0:T(8,128)S(1)}, u32[]{:S(2)}, u32[]{:S(2)}) collective-permute-start(f32[256,1792]{1,0:T(8,128)S(1)} %shard_map.73.refs_0_), channel_id=1, source_target_pairs={{0,1},{1,0},{2,3},{3,2},{4,5},{5,4},{6,7},{7,6},{8,9},{9,8},{10,11... | collective-permute-start | bytes 5505032 | tf_op jit(solution)/shard_map/ppermute | solution.py:249
  65.6 7.7 %copy-start = (f32[256,1792]{1,0:T(8,128)}, f32[256,1792]{1,0:T(8,128)S(1)}, u32[]{:S(2)}) copy-start(f32[256,1792]{1,0:T(8,128)S(1)} %shard_map.77.refs_2_) | copy-start | bytes 5505028
  65.6 26.7 %collective-permute-start.27 = (f32[256,1792]{1,0:T(8,128)S(1)}, f32[256,1792]{1,0:T(8,128)S(1)}, u32[]{:S(2)}, u32[]{:S(2)}) collective-permute-start(f32[256,1792]{1,0:T(8,128)S(1)} %shard_map.77.refs_2_), channel_id=1, source_target_pairs={{0,1},{1,0},{2,3},{3,2},{4,5},{5,4},{6,7},{7,6},{8,9},{9,8},{10,11... | collective-permute-start | bytes 5505032 | tf_op jit(solution)/shard_map/ppermute | solution.py:249
  73.3 19.1 %collective-permute-start.26 = (f32[256,1792]{1,0:T(8,128)S(1)}, f32[256,1792]{1,0:T(8,128)S(1)}, u32[]{:S(2)}, u32[]{:S(2)}) collective-permute-start(f32[256,1792]{1,0:T(8,128)S(1)} %shard_map.76.refs_0_), channel_id=1, source_target_pairs={{0,1},{1,0},{2,3},{3,2},{4,5},{5,4},{6,7},{7,6},{8,9},{9,8},{10,11... | collective-permute-start | bytes 5505032 | tf_op jit(solution)/shard_map/ppermute | solution.py:249
  74.5 1.2 copy-start.4
  88.0 22.4 %collective-permute-start.10 = (bf16[32,2048]{1,0:T(8,128)(2,1)S(1)}, bf16[32,2048]{1,0:T(8,128)(2,1)S(1)}, u32[]{:S(2)}, u32[]{:S(2)}) collective-permute-start(bf16[32,2048]{1,0:T(8,128)(2,1)S(1)} %get-tuple-element.12), channel_id=1, source_target_pairs={{0,4},{4,8},{8,12},{12,14},{14,10},{10,6},{6,2},{2,0},{1,5},{5,9},... | collective-permute-start | bytes 393224 | tf_op jit(solution)/shard_map/ppermute | solution.py:221
  88.9 21.6 %collective-permute-start.14 = (bf16[32,2048]{1,0:T(8,128)(2,1)S(1)}, bf16[32,2048]{1,0:T(8,128)(2,1)S(1)}, u32[]{:S(2)}, u32[]{:S(2)}) collective-permute-start(bf16[32,2048]{1,0:T(8,128)(2,1)S(1)} %get-tuple-element.13), channel_id=1, source_target_pairs={{4,0},{8,4},{12,8},{14,12},{10,14},{6,10},{2,6},{0,2},{5,1},{9,5},... | collective-permute-start | bytes 393224 | tf_op jit(solution)/shard_map/ppermute | solution.py:222
  92.4 1.2 copy-start.5
  105.9 4.6 %copy-start.2 = (f32[224,4096]{1,0:T(8,128)S(1)}, f32[224,4096]{1,0:T(8,128)}, u32[]{:S(2)}) copy-start(f32[224,4096]{1,0:T(8,128)} %get-tuple-element.11) | copy-start | bytes 11010052
  105.9 6.8 %collective-permute-start.28 = (bf16[32,2048]{1,0:T(8,128)(2,1)S(1)}, bf16[32,2048]{1,0:T(8,128)(2,1)S(1)}, u32[]{:S(2)}, u32[]{:S(2)}) collective-permute-start(bf16[32,2048]{1,0:T(8,128)(2,1)S(1)} %get-tuple-element.15), channel_id=1, source_target_pairs={{0,4},{4,8},{8,12},{12,14},{14,10},{10,6},{6,2},{2,0},{1,5},{5,9},... | collective-permute-start | bytes 393224 | tf_op jit(solution)/shard_map/ppermute | solution.py:221
  107.4 5.3 %collective-permute-start.32 = (bf16[32,2048]{1,0:T(8,128)(2,1)S(1)}, bf16[32,2048]{1,0:T(8,128)(2,1)S(1)}, u32[]{:S(2)}, u32[]{:S(2)}) collective-permute-start(bf16[32,2048]{1,0:T(8,128)(2,1)S(1)} %get-tuple-element.16), channel_id=1, source_target_pairs={{4,0},{8,4},{12,8},{14,12},{10,14},{6,10},{2,6},{0,2},{5,1},{9,5},... | collective-permute-start | bytes 393224 | tf_op jit(solution)/shard_map/ppermute | solution.py:222
  108.0 4.7 %copy-start.3 = (f32[224,4096]{1,0:T(8,128)S(1)}, f32[224,4096]{1,0:T(8,128)}, u32[]{:S(2)}) copy-start(f32[224,4096]{1,0:T(8,128)} %get-tuple-element.14) | copy-start | bytes 11010052
  110.5 17.1 %collective-permute-start.15 = (bf16[32,4096]{1,0:T(8,128)(2,1)S(1)}, bf16[32,4096]{1,0:T(8,128)(2,1)S(1)}, u32[]{:S(2)}, u32[]{:S(2)}) collective-permute-start(bf16[32,4096]{1,0:T(8,128)(2,1)S(1)} %pad_maximum_fusion.2), channel_id=1, source_target_pairs={{4,0},{8,4},{12,8},{14,12},{10,14},{6,10},{2,6},{0,2},{5,1},{9,5},... | collective-permute-start | bytes 786440 | tf_op jit(solution)/shard_map/ppermute | solution.py:231
  110.6 9.3 %collective-permute-start.11 = (bf16[32,4096]{1,0:T(8,128)(2,1)S(1)}, bf16[32,4096]{1,0:T(8,128)(2,1)S(1)}, u32[]{:S(2)}, u32[]{:S(2)}) collective-permute-start(bf16[32,4096]{1,0:T(8,128)(2,1)S(1)} %pad_maximum_fusion.1), channel_id=1, source_target_pairs={{0,4},{4,8},{8,12},{12,14},{14,10},{10,6},{6,2},{2,0},{1,5},{5,9},... | collective-permute-start | bytes 786440 | tf_op jit(solution)/shard_map/ppermute | solution.py:230
  112.8 20.6 %collective-permute-start.33 = (bf16[32,4096]{1,0:T(8,128)(2,1)S(1)}, bf16[32,4096]{1,0:T(8,128)(2,1)S(1)}, u32[]{:S(2)}, u32[]{:S(2)}) collective-permute-start(bf16[32,4096]{1,0:T(8,128)(2,1)S(1)} %pad_maximum_fusion.4), channel_id=1, source_target_pairs={{4,0},{8,4},{12,8},{14,12},{10,14},{6,10},{2,6},{0,2},{5,1},{9,5},... | collective-permute-start | bytes 786440 | tf_op jit(solution)/shard_map/ppermute | solution.py:231
  113.7 11.9 %collective-permute-start.29 = (bf16[32,4096]{1,0:T(8,128)(2,1)S(1)}, bf16[32,4096]{1,0:T(8,128)(2,1)S(1)}, u32[]{:S(2)}, u32[]{:S(2)}) collective-permute-start(bf16[32,4096]{1,0:T(8,128)(2,1)S(1)} %pad_maximum_fusion.3), channel_id=1, source_target_pairs={{0,4},{4,8},{8,12},{12,14},{14,10},{10,6},{6,2},{2,0},{1,5},{5,9},... | collective-permute-start | bytes 786440 | tf_op jit(solution)/shard_map/ppermute | solution.py:230
  120.0 11.2 %collective-permute-start.12 = (bf16[32,4096]{1,0:T(8,128)(2,1)S(1)}, bf16[32,4096]{1,0:T(8,128)(2,1)S(1)}, u32[]{:S(2)}, u32[]{:S(2)}) collective-permute-start(bf16[32,4096]{1,0:T(8,128)(2,1)S(1)} %add_convert_fusion.9), channel_id=1, source_target_pairs={{0,4},{4,8},{8,12},{12,14},{14,10},{10,6},{6,2},{2,0},{1,5},{5,9},... | collective-permute-start | bytes 786440 | tf_op jit(solution)/shard_map/ppermute | solution.py:230
  125.6 11.2 %collective-permute-start.30 = (bf16[32,4096]{1,0:T(8,128)(2,1)S(1)}, bf16[32,4096]{1,0:T(8,128)(2,1)S(1)}, u32[]{:S(2)}, u32[]{:S(2)}) collective-permute-start(bf16[32,4096]{1,0:T(8,128)(2,1)S(1)} %add_convert_fusion.4), channel_id=1, source_target_pairs={{0,4},{4,8},{8,12},{12,14},{14,10},{10,6},{6,2},{2,0},{1,5},{5,9},... | collective-permute-start | bytes 786440 | tf_op jit(solution)/shard_map/ppermute | solution.py:230
  131.3 8.8 %collective-permute-start.16 = (bf16[32,4096]{1,0:T(8,128)(2,1)S(1)}, bf16[32,4096]{1,0:T(8,128)(2,1)S(1)}, u32[]{:S(2)}, u32[]{:S(2)}) collective-permute-start(bf16[32,4096]{1,0:T(8,128)(2,1)S(1)} %get-tuple-element.30), channel_id=1, source_target_pairs={{4,0},{8,4},{12,8},{14,12},{10,14},{6,10},{2,6},{0,2},{5,1},{9,5},... | collective-permute-start | bytes 786440 | tf_op jit(solution)/shard_map/ppermute | solution.py:231
  131.4 15.0 %collective-permute-start.13 = (bf16[32,4096]{1,0:T(8,128)(2,1)S(1)}, bf16[32,4096]{1,0:T(8,128)(2,1)S(1)}, u32[]{:S(2)}, u32[]{:S(2)}) collective-permute-start(bf16[32,4096]{1,0:T(8,128)(2,1)S(1)} %get-tuple-element.29), channel_id=1, source_target_pairs={{0,4},{4,8},{8,12},{12,14},{14,10},{10,6},{6,2},{2,0},{1,5},{5,9},... | collective-permute-start | bytes 786440 | tf_op jit(solution)/shard_map/ppermute | solution.py:230
  136.9 9.3 %collective-permute-start.34 = (bf16[32,4096]{1,0:T(8,128)(2,1)S(1)}, bf16[32,4096]{1,0:T(8,128)(2,1)S(1)}, u32[]{:S(2)}, u32[]{:S(2)}) collective-permute-start(bf16[32,4096]{1,0:T(8,128)(2,1)S(1)} %get-tuple-element.34), channel_id=1, source_target_pairs={{4,0},{8,4},{12,8},{14,12},{10,14},{6,10},{2,6},{0,2},{5,1},{9,5},... | collective-permute-start | bytes 786440 | tf_op jit(solution)/shard_map/ppermute | solution.py:231
  137.0 14.9 %collective-permute-start.31 = (bf16[32,4096]{1,0:T(8,128)(2,1)S(1)}, bf16[32,4096]{1,0:T(8,128)(2,1)S(1)}, u32[]{:S(2)}, u32[]{:S(2)}) collective-permute-start(bf16[32,4096]{1,0:T(8,128)(2,1)S(1)} %get-tuple-element.33), channel_id=1, source_target_pairs={{0,4},{4,8},{8,12},{12,14},{14,10},{10,6},{6,2},{2,0},{1,5},{5,9},... | collective-permute-start | bytes 786440 | tf_op jit(solution)/shard_map/ppermute | solution.py:230
  140.2 11.6 %collective-permute-start.17 = (bf16[32,4096]{1,0:T(8,128)(2,1)S(1)}, bf16[32,4096]{1,0:T(8,128)(2,1)S(1)}, u32[]{:S(2)}, u32[]{:S(2)}) collective-permute-start(bf16[32,4096]{1,0:T(8,128)(2,1)S(1)} %add_convert_fusion.6), channel_id=1, source_target_pairs={{4,0},{8,4},{12,8},{14,12},{10,14},{6,10},{2,6},{0,2},{5,1},{9,5},... | collective-permute-start | bytes 786440 | tf_op jit(solution)/shard_map/ppermute | solution.py:231
  146.3 8.3 %collective-permute-start.35 = (bf16[32,4096]{1,0:T(8,128)(2,1)S(1)}, bf16[32,4096]{1,0:T(8,128)(2,1)S(1)}, u32[]{:S(2)}, u32[]{:S(2)}) collective-permute-start(bf16[32,4096]{1,0:T(8,128)(2,1)S(1)} %add_convert_fusion.1), channel_id=1, source_target_pairs={{4,0},{8,4},{12,8},{14,12},{10,14},{6,10},{2,6},{0,2},{5,1},{9,5},... | collective-permute-start | bytes 786440 | tf_op jit(solution)/shard_map/ppermute | solution.py:231
